TPU v7x, 256 devices: a whole 4x4x8 slice. The times are simulated.
256 devices in a mesh: scan: 32 (over z, y), head: 8 (over x, core).
Axes of the slice: x: 4, y: 4, z: 8, core: 2. Of those that a mesh axis runs over, the one named last changes fastest.
Arguments:
- owner_ids: int32 [32768, 1], P('scan'), may hold values from 0 to 31; in each aligned block of 1024 rows (0 to 1023, 1024 to 2047, ...) at most 128 rows name the same one
- owned_points: bfloat16 [512, 135168], P('head', 'scan'), may hold values from -32 to 32
- norm_gain: float32 [512], replicated, may hold values from 0.25 to 1.75
- qkv_weight: bfloat16 [3, 512, 512], P(None, 'head'), may hold values from -5 to 5
- out_weight: bfloat16 [512, 512], P('head'), may hold values from -0.25 to 0.25
- cotangent: bfloat16 [512, 32768], P('head', 'scan'), may hold values from -15 to 15
Outputs:
- mixed_rows: bfloat16 [512, 32768], P('head', 'scan')
- grad_owned: bfloat16 [512, 135168], P('head', 'scan')
- qkv_grad: float32 [3, 512, 512], P(None, 'head', 'scan')
- out_grad: float32 [512, 512], P('head', 'scan')
- gain_grad: float32 [512], P('head')
Inputs may be any that keep to these rules, and one draw needn't show every extreme that they name: `owner_ids`: in each aligned block of 1024 rows (the rows of one index of scan) no owner is named more than 128 times, a bound that some block reaches; every owner is named somewhere.
All inputs are finite; a program needn't handle non-finite values.
Results may differ from a plain program's by a relative error of at most 0.014.
The roundings to bfloat16 on the way count: a program that leaves them out, or rounds other values in their place, can miss the bound.
Values may be sent and summed in bfloat16 or wider, within the bound.
A program may use at most 64 MiB of HBM per device.

v0:
```python
import jax
import jax.numpy as jnp
from jax import lax
from jax.sharding import PartitionSpec as P

HD = 16
P_SIZE = 1024


EPS = 1e-05
PRECISE = lax.Precision.HIGHEST


def prefix(part, axis, combine, identity):
    place = lax.axis_index(axis)
    gathered = lax.all_gather(part, axis)
    state = jnp.zeros_like(part) + jnp.asarray(identity, part.dtype)

    def one(hop, state):
        return combine(state, lax.dynamic_index_in_dim(gathered, hop, 0, False))

    return lax.fori_loop(0, place, one, state)


def heads_first(matrix, patches):
    local_heads = matrix.shape[0] // HD
    return (
        matrix.reshape(local_heads, HD, patches, P_SIZE)
        .transpose(2, 0, 1, 3)
        .reshape(patches * local_heads, HD, P_SIZE)
    )


def rows_first(tensor, patches):
    local_heads = tensor.shape[0] // patches
    return (
        tensor.reshape(patches, local_heads, HD, P_SIZE)
        .transpose(1, 2, 0, 3)
        .reshape(local_heads * HD, patches * P_SIZE)
    )


def attend_item(queries, key_rows, values):
    span_width = min(512, P_SIZE)
    outputs = []
    for block_start in range(0, P_SIZE, span_width):
        chosen = queries[:, block_start : block_start + span_width]
        scores = jnp.einsum("dq,dk->qk", chosen, key_rows, precision=PRECISE) * HD ** (-0.5)
        row_peak = jnp.max(scores, axis=1, keepdims=True)
        weights = jnp.exp(scores - row_peak)
        weights = weights / jnp.sum(weights, axis=1, keepdims=True)
        outputs.append(jnp.einsum("qk,dk->dq", weights, values, precision=PRECISE))
    return jnp.concatenate(outputs, axis=1)


def attend_back(queries, key_rows, values, grad_heads):
    span_width = min(512, P_SIZE)
    key_grad = jnp.zeros_like(key_rows)
    value_grad = jnp.zeros_like(values)
    query_parts = []
    for block_start in range(0, P_SIZE, span_width):
        chosen = queries[:, block_start : block_start + span_width]
        chosen_grad = grad_heads[:, block_start : block_start + span_width]
        scores = jnp.einsum("dq,dk->qk", chosen, key_rows, precision=PRECISE) * HD ** (-0.5)
        row_peak = jnp.max(scores, axis=1, keepdims=True)
        weights = jnp.exp(scores - row_peak)
        weights = weights / jnp.sum(weights, axis=1, keepdims=True)
        value_grad = value_grad + jnp.einsum("qk,dq->dk", weights, chosen_grad, precision=PRECISE)
        weight_grad = jnp.einsum("dq,dk->qk", chosen_grad, values, precision=PRECISE)
        center = jnp.sum(weights * weight_grad, axis=1, keepdims=True)
        score_grad = weights * (weight_grad - center) * HD ** (-0.5)
        query_parts.append(jnp.einsum("qk,dk->dq", score_grad, key_rows, precision=PRECISE))
        key_grad = key_grad + jnp.einsum("qk,dq->dk", score_grad, chosen, precision=PRECISE)
    return (jnp.concatenate(query_parts, axis=1), key_grad, value_grad)


def per_device(owner_ids, owned_points, norm_gain, qkv_weight, out_weight, cotangent):
    scan_count = lax.axis_size("scan")
    row_count = owner_ids.shape[0]
    local_width = qkv_weight.shape[1]
    patches = row_count // P_SIZE
    slot_count = owned_points.shape[1]
    bucket = slot_count // (scan_count + 1)
    owners = owner_ids[:, 0]
    onehot = (owners[:, None] == jnp.arange(scan_count, dtype=jnp.int32)[None, :]).astype(jnp.int32)
    running = jnp.cumsum(onehot, axis=0) - onehot
    rank_local = jnp.sum(running * onehot, axis=1)
    tallies = jnp.sum(onehot, axis=0)
    before = prefix(
        tallies, "scan", lambda earlier, later: earlier + later, jnp.zeros_like(tallies)
    )
    starts, sizes_from = (
        lax.all_to_all(before[:, None], "scan", split_axis=0, concat_axis=0, tiled=True),
        lax.all_to_all(tallies[:, None], "scan", split_axis=0, concat_axis=0, tiled=True),
    )
    send_rows = jax.vmap(
        lambda offset_start: lax.dynamic_slice_in_dim(owned_points, offset_start, bucket, 1)
    )(starts[:, 0])
    arrived = lax.all_to_all(send_rows, "scan", split_axis=0, concat_axis=0, tiled=True)
    regrouped = arrived[owners, :, rank_local].T
    full_rows = lax.all_gather(regrouped, "head", axis=0, tiled=True)
    channels = full_rows.shape[0]
    head_slot = lax.axis_index("head")
    floats = full_rows.astype(jnp.float32)
    row_mean = jnp.mean(floats, axis=0, keepdims=True)
    centered = floats - row_mean
    inv_scale = lax.rsqrt(jnp.mean(centered * centered, axis=0, keepdims=True) + EPS)
    normed = centered * inv_scale
    scaled = (normed * norm_gain[:, None]).astype(jnp.bfloat16)
    triple = jnp.einsum("cr,iwc->iwr", scaled, qkv_weight, preferred_element_type=jnp.float32)
    query_heads = heads_first(triple[0], patches)
    key_heads = heads_first(triple[1], patches)
    value_heads = heads_first(triple[2], patches)
    context = lax.map(
        lambda item_triple: attend_item(*item_triple), (query_heads, key_heads, value_heads)
    )
    context_b = rows_first(context, patches).astype(jnp.bfloat16)
    branch_full = jnp.einsum("wc,wr->cr", out_weight, context_b, preferred_element_type=jnp.float32)
    branch_local = lax.psum_scatter(
        branch_full.astype(jnp.bfloat16), "head", scatter_dimension=0, tiled=True
    ).astype(jnp.float32)
    mixed_rows = (regrouped.astype(jnp.float32) + branch_local).astype(jnp.bfloat16)
    cot_piece = lax.all_gather(cotangent, "head", axis=0, tiled=True)
    grad_out = jnp.zeros((local_width, channels), jnp.float32)
    grad_context = jnp.einsum(
        "wc,cr->wr", out_weight, cot_piece, preferred_element_type=jnp.float32
    )
    piece_grad = jnp.einsum("wr,cr->wc", context_b, cot_piece, preferred_element_type=jnp.float32)
    grad_out = lax.dynamic_update_slice_in_dim(grad_out, piece_grad, jnp.int32(0), 1)
    grad_context, out_grad_local = (grad_context, grad_out)
    out_grad = lax.psum_scatter(out_grad_local, "scan", scatter_dimension=1, tiled=True)
    grad_heads = heads_first(grad_context, patches)
    query_grad, key_grad, value_grad = lax.map(
        lambda item_four: attend_back(*item_four), (query_heads, key_heads, value_heads, grad_heads)
    )
    grads_b = jnp.stack(
        [
            rows_first(query_grad, patches),
            rows_first(key_grad, patches),
            rows_first(value_grad, patches),
        ]
    ).astype(jnp.bfloat16)
    qkv_grad_local = jnp.einsum("iwr,cr->iwc", grads_b, scaled, preferred_element_type=jnp.float32)
    qkv_grad = lax.psum_scatter(qkv_grad_local, "scan", scatter_dimension=2, tiled=True)
    partial_input = jnp.einsum(
        "iwc,iwr->cr", qkv_weight, grads_b, preferred_element_type=jnp.float32
    )
    normed_local = lax.dynamic_slice_in_dim(normed, head_slot * local_width, local_width, 0)
    normed_grad_full = lax.psum(partial_input.astype(jnp.bfloat16), "head").astype(jnp.float32)
    weighted = normed_grad_full * norm_gain[:, None]
    mean_first = jnp.mean(weighted, axis=0, keepdims=True)
    mean_second = jnp.mean(weighted * normed, axis=0, keepdims=True)
    input_full = inv_scale * (weighted - mean_first - normed * mean_second)
    input_local = lax.dynamic_slice_in_dim(input_full, head_slot * local_width, local_width, 0)
    normed_grad = lax.dynamic_slice_in_dim(
        normed_grad_full, head_slot * local_width, local_width, 0
    )
    grad_points = (cotangent.astype(jnp.float32) + input_local).astype(jnp.bfloat16)
    gain_grad = lax.psum(jnp.sum(normed_grad * normed_local, axis=1), "scan")
    send_back = (
        jnp.zeros((scan_count, local_width, bucket), jnp.bfloat16)
        .at[owners, :, rank_local]
        .set(grad_points.T)
    )
    returned = lax.all_to_all(send_back, "scan", split_axis=0, concat_axis=0, tiled=True)
    within = jnp.arange(bucket, dtype=jnp.int32)[None, :]
    slot_target = jnp.where(within < sizes_from, starts + within, slot_count).reshape(-1)
    flat_returned = returned.transpose(1, 0, 2).reshape(local_width, scan_count * bucket)
    grad_owned = jnp.zeros_like(owned_points).at[:, slot_target].set(flat_returned, mode="drop")
    return (mixed_rows, grad_owned, qkv_grad, out_grad, gain_grad)


def solution(mesh):
    in_specs = (
        P("scan", None),
        P("head", "scan"),
        P(),
        P(None, "head", None),
        P("head", None),
        P("head", "scan"),
    )
    out_specs = (
        P("head", "scan"),
        P("head", "scan"),
        P(None, "head", "scan"),
        P("head", "scan"),
        P("head"),
    )
    return jax.shard_map(
        per_device, mesh=mesh, in_specs=in_specs, out_specs=out_specs, check_vma=False
    )
```

profile of v0, /device:TPU:1, one launch (start us, length us, event | category | flops | bytes accessed | tf_op | source)
XLA Modules:
  0.0 821.4 jit_solution(3774519046148898443)
XLA Ops:
  8.0 9.0 %reduce-window.6 = s32[32,8,128]{2,1,0:T(8,128)S(1)} reduce-window(s32[32,8,128]{2,1,0:T(8,128)S(1)} %fusion.103, s32[]{:T(128)} %constant.75.clone.1), window={size=1x1x128 pad=0_0x0_0x127_0}, to_apply=%region_3.4 | reduce-window | flops 4161536 | bytes 262148 | tf_op jit(solution)/shard_map/reduce-window
  20.4 20.0 %all-reduce.1 = s32[1024]{0:T(1024)S(1)} all-reduce(s32[1024]{0:T(1024)S(1)} %dynamic-update-slice.2), channel_id=2, replica_groups=mesh['scan'=32,'head'=8] {'scan'}, use_global_device_ids=true, to_apply=%add.1 | all-reduce | flops 1024 | bytes 8192
  41.2 4.3 all-to-all-start
  46.3 7.8 all-to-all-done
  54.7 85.8 %while.38 = (s32[]{:T(128)}, bf16[64,4224]{1,0:T(8,128)(2,1)}, s32[32,2]{0,1:T(2,128)S(1)}, bf16[32,64,128]{2,1,0:T(8,128)(2,1)}, s32[]{:T(128)}) while((s32[]{:T(128)}, bf16[64,4224]{1,0:T(8,128)(2,1)}, s32[32,2]{0,1:T(2,128)S(1)}, bf16[32,64,128]{2,1,0:T(8,128)(2,1)}, s32[]{:T(128)}) %tuple.98), condition=%wide.while_cond, body=%wide.while_body.sunk | while | flops 2 | bytes 33381 | solution.py:97
  71.4 2.1 bitcast_dynamic-update-slice_fusion.2
  140.5 3.9 all-to-all-start.1
  144.5 12.9 %all-to-all-done.1 = bf16[32,64,128]{2,1,0:T(8,128)(2,1)S(1)} async-done(((bf16[32,64,128]{2,1,0:T(8,128)(2,1)}), bf16[32,64,128]{2,1,0:T(8,128)(2,1)S(1)}, u32[]{:S(2)}, u32[]{:S(2)}) %all-to-all-start.1) | async-done | bytes 524320 | tf_op jit(solution)/shard_map/all_to_all | solution.py:99
  157.9 5.8 gather_fusion
  165.3 3.8 all-to-all-start.2
  170.9 22.6 %all-gather.4.cloned.1.call-done = bf16[512,1024]{1,0:T(8,128)(2,1)} async-done(((bf16[64,1024]{1,0:T(8,128)(2,1)}), bf16[512,1024]{1,0:T(8,128)(2,1)}) %all-gather.4.cloned.1.call-update) | async-done | bytes 1048592 | tf_op jit(solution)/shard_map/all_gather | solution.py:101
  196.6 83.5 %while.37 = (s32[]{:T(128)}, bf16[4,16,1024]{2,1,0:T(8,128)(2,1)S(1)}, bf16[4,16,1024]{2,1,0:T(8,128)(2,1)S(1)}, bf16[4,16,1024]{2,1,0:T(8,128)(2,1)S(1)}, f32[4...) while((s32[]{:T(128)}, ...), condition=%wide.region_22.23_spmd, body=%wide.region_15.22_spmd.sunk | while | flops 1023505408 | bytes 43384972 | solution.py:133
  199.6 2.3 multiply_reduce_fusion.20
  208.8 2.3 multiply_reduce_fusion.18
  218.2 2.3 multiply_reduce_fusion.20
  227.4 2.3 multiply_reduce_fusion.18
  236.8 2.3 multiply_reduce_fusion.20
  246.0 2.3 multiply_reduce_fusion.18
  255.4 2.3 multiply_reduce_fusion.20
  264.7 2.3 multiply_reduce_fusion.18
  281.8 37.1 %while.36 = (s32[]{:T(128)}, bf16[4,16,1024]{2,1,0:T(8,128)(2,1)S(1)}, f32[4,16,1024]{2,1,0:T(8,128)S(1)}, f32[4,16,1024]{2,1,0:T(8,128)S(1)}, f32[4,16,1024]{2,1,0:T(8,128)S(1)}, /*index=5*/s32[]{:T(128)}) while((s32[]{:T(128)}, bf16[4,16,1024]{2,1,0:T(8,128)(2,1)S(1)}, f32[4,16,1024]{2,1,0:T(8,128)S(1)}, f32[4,16,1024]{2,1,0:T(8,128)S(1)}, ...), condition=%wide.region_13.14_spmd, body=%wide.region_8.13_spmd.sunk | while | flops 411105280 | bytes 13160549 | solution.py:114
  322.3 24.6 %all-reduce.4.cloned.1.call-done = bf16[512,1024]{0,1:T(8,128)(2,1)} async-done(((bf16[512,1024]{0,1:T(8,128)(2,1)}), bf16[512,1024]{0,1:T(8,128)(2,1)}) %all-reduce.4.cloned.1.call-update) | async-done | bytes 1048592 | tf_op jit(solution)/shard_map/psum | solution.py:149
  346.9 3.1 fusion.92
  350.1 5.6 scatter_custom_fusion.1
  355.6 2.3 copy.47
  358.0 9.7 %all-to-all-start.3 = ((bf16[32,64,128]{2,1,0:T(8,128)(2,1)}), bf16[32,64,128]{2,1,0:T(8,128)(2,1)}, u32[]{:S(2)}, u32[]{:S(2)}) async-start(bf16[32,64,128]{2,1,0:T(8,128)(2,1)} %bitcast.182), calls=%async_computation.3 | async-start | bytes 1048576 | tf_op jit(solution)/shard_map/all_to_all | solution.py:165
  367.8 2.4 fusion.112
  370.2 3.0 fusion.98
  375.1 60.8 %psum.15 = f32[64]{0:T(128)} all-reduce(f32[64]{0:T(128)S(1)} %multiply_reduce_fusion.7), channel_id=1, replica_groups=mesh['scan'=32,'head'=8] {'scan'}, use_global_device_ids=true, to_apply=%region_31.32 | all-reduce | flops 64 | bytes 512 | tf_op jit(solution)/shard_map/psum | solution.py:159
  437.5 11.2 %scatter_custom_fusion = bf16[64,4224]{0,1:T(8,128)(2,1)S(1)} fusion(s32[4096]{0:T(1024)S(1)} %bitcast.200, bf16[4096,64]{1,0:T(8,128)(2,1)S(1)} %copy.49, bf16[]{:T(256)} %constant.84.clone.1), kind=kCustom, calls=%fused_computation.117 | custom fusion | bytes 540674 | tf_op jit(solution)/shard_map/scatter | solution.py:169
  452.2 144.3 %reduce-scatter.8.cloned.1.call-done = f32[64,16]{0,1:T(8,128)} async-done(((f32[64,512]{0,1:T(8,128)}), f32[64,16]{0,1:T(8,128)}) %reduce-scatter.8.cloned.1.call-update) | async-done | bytes 4112 | tf_op jit(solution)/shard_map/reduce_scatter | solution.py:131
  596.4 217.9 %reduce-scatter.6.cloned.1.call-done = f32[3,64,16]{1,2,0:T(8,128)} async-done(((f32[3,64,512]{1,2,0:T(8,128)}), f32[3,64,16]{1,2,0:T(8,128)}) %reduce-scatter.6.cloned.1.call-update) | async-done | bytes 12304 | tf_op jit(solution)/shard_map/reduce_scatter | solution.py:144
  (269 shorter events, 200.9 us)
Async XLA Ops:
  7.2 188.6 %copy-start = (bf16[3,64,512]{2,1,0:T(8,128)(2,1)S(1)}, bf16[3,64,512]{2,1,0:T(8,128)(2,1)}, u32[]{:S(2)}) copy-start(bf16[3,64,512]{2,1,0:T(8,128)(2,1)} %param.15) | copy-start | bytes 589828
  7.2 137.3 %copy-start.8 = (s32[1024,1]{0,1:T(1,128)S(1)}, s32[1024,1]{0,1:T(1,128)}, u32[]{:S(2)}) copy-start(s32[1024,1]{0,1:T(1,128)} %param.12) | copy-start | bytes 12292
  41.2 12.8 %all-to-all-start = ((s32[32,1,1]{2,1,0:T(1,128)}), s32[32,1,1]{2,1,0:T(1,128)S(1)}, u32[]{:S(2)}, u32[]{:S(2)}) async-start(s32[32,1,1]{2,1,0:T(1,128)} %copy.38), calls=%async_computation | async-start | bytes 32768 | tf_op jit(solution)/shard_map/all_to_all | solution.py:93
  45.6 123.8 %all-gather.6.cloned.1.call-start = ((), (), s32[]{:S(2)}) async-start(), calls=%async_computation.8 | async-start | bytes 1179648 | tf_op jit(solution)/shard_map/all_gather | solution.py:123
  140.5 16.8 %all-to-all-start.1 = ((bf16[32,64,128]{2,1,0:T(8,128)(2,1)}), bf16[32,64,128]{2,1,0:T(8,128)(2,1)S(1)}, u32[]{:S(2)}, u32[]{:S(2)}) async-start(bf16[32,64,128]{2,1,0:T(8,128)(2,1)} %get-tuple-element.111), calls=%async_computation.1 | async-start | bytes 1048576 | tf_op jit(solution)/shard_map/all_to_all | solution.py:99
  144.4 49.1 %all-gather.4.cloned.1.call-start = ((), (), s32[]{:S(2)}) async-start(), calls=%async_computation.7 | async-start | bytes 1179648 | tf_op jit(solution)/shard_map/all_gather | solution.py:101
  157.9 11.3 %copy-start.11 = (s32[2]{0:T(128)S(1)}, s32[2]{0:T(128)}, u32[]{:S(2)}) copy-start(s32[2]{0:T(128)} %constant.90) | copy-start | bytes 28
  157.9 11.4 %copy-start.10 = (s32[2]{0:T(128)S(1)}, s32[2]{0:T(128)}, u32[]{:S(2)}) copy-start(s32[2]{0:T(128)} %constant.93) | copy-start | bytes 28
  157.9 11.5 %copy-start.4 = (bf16[64,512]{1,0:T(8,128)(2,1)S(1)}, bf16[64,512]{1,0:T(8,128)(2,1)}, u32[]{:S(2)}) copy-start(bf16[64,512]{1,0:T(8,128)(2,1)} %param.16) | copy-start | bytes 196612
  163.8 31.5 %copy-start.1 = (bf16[1024,64]{1,0:T(8,128)(2,1)}, bf16[1024,64]{1,0:T(8,128)(2,1)S(1)}, u32[]{:S(2)}) copy-start(bf16[1024,64]{1,0:T(8,128)(2,1)S(1)} %gather_fusion) | copy-start | bytes 393220
  165.3 156.3 %all-to-all-start.2 = ((s32[32,1,1]{2,1,0:T(1,128)}), s32[32,1,1]{2,1,0:T(1,128)S(1)}, u32[]{:S(2)}, u32[]{:S(2)}) async-start(s32[32,1,1]{2,1,0:T(1,128)} %copy.45), calls=%async_computation.2 | async-start | bytes 32768 | tf_op jit(solution)/shard_map/all_to_all | solution.py:94
  169.1 177.8 %all-reduce.4.cloned.1.call-start = ((), (), s32[]{:S(2)}) async-start(), calls=%async_computation.9 | async-start | bytes 2097152 | tf_op jit(solution)/shard_map/psum | solution.py:149
  170.9 24.9 %copy-start.9 = (f32[512]{0:T(512)S(1)}, f32[512]{0:T(512)}, u32[]{:S(2)}) copy-start(f32[512]{0:T(512)} %param.14) | copy-start | bytes 6148
  280.2 1.6 copy-start.5
  280.2 1.6 copy-start.6
  280.2 1.6 copy-start.7
  281.7 168.5 %reduce-scatter.10.cloned.1.call-start = ((), (), s32[]{:S(2)}) async-start(), calls=%async_computation.12 | async-start | bytes 1179648
  318.9 1.8 copy-start.3
  358.0 77.9 %all-to-all-start.3 = ((bf16[32,64,128]{2,1,0:T(8,128)(2,1)}), bf16[32,64,128]{2,1,0:T(8,128)(2,1)}, u32[]{:S(2)}, u32[]{:S(2)}) async-start(bf16[32,64,128]{2,1,0:T(8,128)(2,1)} %bitcast.182), calls=%async_computation.3 | async-start | bytes 1048576 | tf_op jit(solution)/shard_map/all_to_all | solution.py:165
  367.7 228.7 %reduce-scatter.8.cloned.1.call-start = ((), (), s32[]{:S(2)}) async-start(), calls=%async_computation.11 | async-start | bytes 270336 | tf_op jit(solution)/shard_map/reduce_scatter | solution.py:131
  370.2 444.2 %reduce-scatter.6.cloned.1.call-start = ((), (), s32[]{:S(2)}) async-start(), calls=%async_computation.10 | async-start | bytes 811008 | tf_op jit(solution)/shard_map/reduce_scatter | solution.py:144
  437.0 14.3 %copy-start.2 = (bf16[1024,64]{1,0:T(8,128)(2,1)S(1)}, bf16[1024,64]{1,0:T(8,128)(2,1)}, u32[]{:S(2)}) copy-start(bf16[1024,64]{1,0:T(8,128)(2,1)} %copy-done.1) | copy-start | bytes 393220
Sparse Core Ops, SparseCore 0:
  48.3 32.2 all-gather.5
  164.7 28.7 all-gather.3
  281.8 65.0 all-reduce.3
  349.3 33.6 reduce-scatter.9
  387.3 209.1 reduce-scatter.7
  601.2 213.1 reduce-scatter.5
where the time goes:
time: 834 us; the launch traced here: 821 us
  waiting for transfers between devices  431 us (52%)
  local copies, waits for them, and re-layouts  119 us (14%)
  matrix products  112 us (13%)
  blocking collectives  80.8 us (10%)
  other arithmetic  32.2 us (4%)
  starting transfers between devices  22 us (3%)
  between operations  15.5 us (2%)
  loops' own time  9.42 us (1%)
    reduce_scatter x1, waiting for transfers between devices, per_device(): lax.psum_scatter(qkv_grad_local, 'scan', scatter_dimension=2, tiled=True)  218 us
    reduce_scatter x1, waiting for transfers between devices, per_device(): lax.psum_scatter(out_grad_local, 'scan', scatter_dimension=1, tiled=True)  144 us
    gather x96, local copies, waits for them, and re-layouts  85.7 us
    psum x1, blocking collectives, per_device(): gain_grad = lax.psum(jnp.sum(normed_grad * normed_local, axis=1), 'scan')  60.8 us
    psum x1, waiting for transfers between devices, per_device(): lax.psum(partial_input.astype(jnp.bfloat16), 'head').astype(jnp.float32)  24.6 us
    all_gather x1, waiting for transfers between devices, per_device(): full_rows = lax.all_gather(regrouped, 'head', axis=0, tiled=True)  22.6 us
    unnamed x1, blocking collectives  20 us
    dot_general x8, matrix products, attend_back(): jnp.einsum('dq,dk->qk', chosen_grad, values, precision=PRECISE)  18.6 us
  transfers between devices with their start and end apart: 10, of which 6 were waited for; matrix products, arithmetic and copies ran while one was open for 30% of the time, Pallas kernels for 0%

commit v1 on v0

v1 whole, which is shorter than its diff:
```python
import functools

import jax
import jax.numpy as jnp
from jax import lax
from jax.experimental import pallas as pl
from jax.experimental.pallas import tpu as pltpu
from jax.sharding import PartitionSpec as P

HD = 16
BUCKET = 128
EPS = 1e-05
SPAN = 256
LOG2E = 1.4426950408889634
MESH = pl.DeviceIdType.MESH
F32 = jnp.float32
BF16 = jnp.bfloat16
VMEM = pl.BlockSpec(memory_space=pltpu.VMEM)
SMEM = pl.BlockSpec(memory_space=pltpu.SMEM)
LIMIT = 56 * 1024 * 1024


def dot_nn(a, b):
    return lax.dot_general(a, b, (((1,), (0,)), ((), ())), preferred_element_type=F32)


def dot_nt(a, b):
    return lax.dot_general(a, b, (((1,), (1,)), ((), ())), preferred_element_type=F32)


def dot_tn(a, b):
    return lax.dot_general(a, b, (((0,), (0,)), ((), ())), preferred_element_type=F32)


def split2(x):
    high = x.astype(BF16)
    return high, (x - high.astype(F32)).astype(BF16)


def split3(x):
    high = x.astype(BF16)
    rest = x - high.astype(F32)
    middle = rest.astype(BF16)
    return high, middle, (rest - middle.astype(F32)).astype(BF16)


def left_stack(x):
    a, b, c = split3(x)
    return [a, b, a, b, c, a]


def right_stack(x):
    a, b, c = split3(x)
    return [a, a, b, b, a, c]


def greet(ns, nh, scan, head):
    s, h = lax.axis_index("scan"), lax.axis_index("head")
    barrier = pltpu.get_barrier_semaphore()
    count = 0
    if scan:
        count += ns - 1

        def along_scan(j, carry):
            pl.semaphore_signal(
                barrier, inc=1, device_id=(lax.rem(s + j, ns), h), device_id_type=MESH
            )
            return carry

        lax.fori_loop(1, ns, along_scan, 0)
    if head:
        count += nh - 1

        def along_head(j, carry):
            pl.semaphore_signal(
                barrier, inc=1, device_id=(s, lax.rem(h + j, nh)), device_id_type=MESH
            )
            return carry

        lax.fori_loop(1, nh, along_head, 0)
    return barrier, count


def tally_kernel(ns, owner_ref, code_ref, sizes_ref, tall, send_sem, recv_sem):
    s, h = lax.axis_index("scan"), lax.axis_index("head")
    barrier, count = greet(ns, 1, True, False)
    owners = owner_ref[...]
    rows = owners.shape[1]
    hot = lax.broadcasted_iota(jnp.int32, (ns, rows), 0) == owners
    ones = jnp.where(hot, 1.0, 0.0)
    total = jnp.sum(ones, axis=1, keepdims=True).astype(jnp.int32)
    tall[...] = jnp.broadcast_to(total, (ns, 128))
    pl.semaphore_wait(barrier, count)

    def copy(j):
        peer = lax.rem(s + j, ns)
        return pltpu.make_async_remote_copy(
            src_ref=tall.at[pl.ds(peer, 1), :],
            dst_ref=sizes_ref.at[pl.ds(s, 1), :],
            send_sem=send_sem.at[j],
            recv_sem=recv_sem.at[j],
            device_id=(peer, h),
            device_id_type=MESH,
        )

    def start(j, carry):
        copy(j).start()
        return carry

    lax.fori_loop(1, ns, start, 0)
    sizes_ref[pl.ds(s, 1), :] = tall[pl.ds(s, 1), :]
    before = jnp.where(
        lax.broadcasted_iota(jnp.int32, (128, 128), 0)
        < lax.broadcasted_iota(jnp.int32, (128, 128), 1),
        1.0,
        0.0,
    ).astype(BF16)
    carried = jnp.zeros((ns, 1), F32)
    for b in range(0, rows, 128):
        part = ones[:, b : b + 128]
        running = dot_nn(part.astype(BF16), before) + carried
        rank = jnp.sum(running * part, axis=0, keepdims=True)
        code_ref[:, b : b + 128] = owners[:, b : b + 128] * BUCKET + rank.astype(jnp.int32)
        carried = carried + jnp.sum(part, axis=1, keepdims=True)

    def finish(j, carry):
        copy(j).wait()
        return carry

    lax.fori_loop(1, ns, finish, 0)


def window_kernel(ns, sizes_ref, points_ref, out_ref):
    def one(d, begin):
        tile = begin // 128
        off = begin - tile * 128
        window = points_ref[:, pl.ds(pl.multiple_of(tile * 128, 128), 256)].astype(F32)
        rolled = pltpu.roll(window, lax.rem(256 - off, 256), 1)
        out_ref[d] = rolled[:, :128].astype(BF16)
        return begin + sizes_ref[d, 0]

    lax.fori_loop(0, ns, one, jnp.int32(0))


def hot_block(code, first, height):
    ids = lax.broadcasted_iota(jnp.int32, (height, code.shape[1]), 0) + first
    return jnp.where(ids == code, 1.0, 0.0).astype(BF16)


def gather_kernel(
    ns, nh, send_ref, code_ref, cot_ref, full_ref, cotfull_ref,
    arrived, hots, far_send, far_recv, near_send, near_recv,
):
    s, h = lax.axis_index("scan"), lax.axis_index("head")
    width = send_ref.shape[1]
    nx = nh // 2
    x, core = h // 2, lax.rem(h, 2)
    twin = x * 2 + 1 - core
    barrier, count = greet(ns, nh, True, True)
    pl.semaphore_wait(barrier, count)

    def far(j):
        peer = lax.rem(s + j, ns)
        return pltpu.make_async_remote_copy(
            src_ref=send_ref.at[peer],
            dst_ref=arrived.at[s],
            send_sem=far_send.at[j],
            recv_sem=far_recv.at[j],
            device_id=(peer, h),
            device_id_type=MESH,
        )

    def far_start(j, carry):
        far(j).start()
        return carry

    def push(which, ref, piece, slot, to):
        block = ref.at[pl.ds(pl.multiple_of(piece * width, width), width), :]
        return pltpu.make_async_remote_copy(
            src_ref=block,
            dst_ref=block,
            send_sem=near_send.at[which, slot],
            recv_sem=near_recv.at[which, piece],
            device_id=(s, to),
            device_id_type=MESH,
        )

    def spread(which, ref):
        for j in range(1, nx):
            push(which, ref, h, j, lax.rem(x + j, nx) * 2 + core).start()
        push(which, ref, h, 0, twin).start()

    def relay(which, ref):
        for j in range(1, nx):
            piece = lax.rem(x + nx - j, nx) * 2 + core
            push(which, ref, piece, nx + j, twin).wait_recv()
            push(which, ref, piece, nx + j, twin).start()

    def settle(which, ref):
        for j in range(1, nx):
            push(which, ref, h, j, twin).wait_send()
            push(which, ref, h, nx + j, twin).wait_send()
        push(which, ref, h, 0, twin).wait_send()
        for j in range(nx):
            piece = lax.rem(x + nx - j, nx) * 2 + 1 - core
            push(which, ref, piece, 0, twin).wait_recv()

    mine = pl.ds(pl.multiple_of(h * width, width), width)
    lax.fori_loop(1, ns, far_start, 0)
    cotfull_ref[mine, :] = cot_ref[...]
    spread(0, cotfull_ref)
    arrived[pl.ds(s, 1)] = send_ref[pl.ds(s, 1)]
    code = code_ref[...]

    def build(i, carry):
        first = pl.multiple_of(i * 256, 256)
        hots[pl.ds(first, 256), :] = hot_block(code, first, 256)
        return carry

    lax.fori_loop(0, ns // 2, build, 0)
    relay(0, cotfull_ref)

    def far_finish(j, carry):
        far(j).wait()
        return carry

    lax.fori_loop(1, ns, far_finish, 0)
    total = jnp.zeros((width, code.shape[1]), F32)
    for i in range(ns // 4):
        pieces = jnp.concatenate([arrived[4 * i + t] for t in range(4)], axis=1)
        total = total + dot_nn(pieces, hots[512 * i : 512 * (i + 1), :])
    full_ref[mine, :] = total.astype(BF16)
    spread(1, full_ref)
    relay(1, full_ref)
    settle(0, cotfull_ref)
    settle(1, full_ref)


def block_kernel(
    full_ref, cot_ref, gain_ref, weight_ref, outw_ref, head_ref,
    branch_ref, part_ref, stats_ref, wgrad_ref, own_ref, normown_ref, gainown_ref,
    normed, scaled, query, keys, value, gradc, context, grads, key_t, value_t,
):
    channels, rows = full_ref.shape
    width = outw_ref.shape[0]
    gain = jnp.transpose(jnp.broadcast_to(gain_ref[...], (8, channels)))[:, :1]
    floats = full_ref[...].astype(F32)
    mean = jnp.sum(floats, axis=0, keepdims=True) * (1.0 / channels)
    centered = floats - mean
    inv = lax.rsqrt(jnp.sum(centered * centered, axis=0, keepdims=True) * (1.0 / channels) + EPS)
    normed[...] = centered * inv
    scaled[...] = (normed[...] * gain).astype(BF16)
    for i, ref in enumerate((query, keys, value)):
        ref[...] = dot_nn(weight_ref[i], scaled[...])
    gradc[...] = dot_nn(outw_ref[...], cot_ref[...])

    def one_head(head, carry):
        at = pl.ds(pl.multiple_of(head * HD, HD), HD)
        q, k, v, g = query[at, :], keys[at, :], value[at, :], gradc[at, :]
        key_t[...] = jnp.transpose(jnp.concatenate(left_stack(k), axis=0))
        ones = jnp.ones((HD, rows), BF16)
        value_t[...] = jnp.transpose(jnp.concatenate(left_stack(v) + [ones], axis=0))
        v_rows = jnp.concatenate(list(split2(v)) + [ones], axis=0)
        k_rows = jnp.concatenate(list(split2(k)), axis=0)
        key_grad = jnp.zeros((HD * 2, rows), F32)
        value_grad = jnp.zeros((HD * 2, rows), F32)
        for b in range(0, rows, SPAN):
            qb, gb = q[:, b : b + SPAN], g[:, b : b + SPAN]
            q_stack = jnp.concatenate(right_stack(qb * (HD**-0.5 * LOG2E)), axis=0)
            scores = dot_nn(key_t[...], q_stack)
            peak = jnp.max(scores, axis=0, keepdims=True)
            weights = jnp.exp2(scores - peak).astype(BF16)
            sums = dot_nn(v_rows, weights)
            share = 1.0 / sums[2 * HD : 2 * HD + 1]
            ctx = (sums[:HD] + sums[HD : 2 * HD]) * share
            context[at, b : b + SPAN] = ctx.astype(BF16)
            gs = gb * share
            center = jnp.sum(gs * ctx, axis=0, keepdims=True) * (-(HD**-0.5))
            parts = [jnp.broadcast_to(t, (HD, SPAN)).astype(F32) for t in split3(center)]
            row = lax.broadcasted_iota(jnp.int32, (HD, SPAN), 0)
            tail = jnp.where(
                row == 0, parts[0], jnp.where(row == 1, parts[1], jnp.where(row == 2, parts[2], 0.0))
            ).astype(BF16)
            g_stack = jnp.concatenate(right_stack(gs * HD**-0.5) + [tail], axis=0)
            delta = dot_nn(value_t[...], g_stack)
            score_grad = (weights.astype(F32) * delta).astype(BF16)
            value_grad = value_grad + dot_nt(jnp.concatenate(list(split2(gs)), axis=0), weights)
            dq = dot_nn(k_rows, score_grad)
            grads[at, b : b + SPAN] = (dq[:HD] + dq[HD:]).astype(BF16)
            key_grad = key_grad + dot_nt(jnp.concatenate(list(split2(qb)), axis=0), score_grad)
        k_at = pl.ds(pl.multiple_of(width + head * HD, HD), HD)
        v_at = pl.ds(pl.multiple_of(2 * width + head * HD, HD), HD)
        grads[k_at, :] = (key_grad[:HD] + key_grad[HD:]).astype(BF16)
        grads[v_at, :] = (value_grad[:HD] + value_grad[HD:]).astype(BF16)
        return carry

    lax.fori_loop(0, width // HD, one_head, 0)
    branch_ref[...] = dot_tn(outw_ref[...], context[...]).astype(BF16)
    wgrad_ref[:, : 3 * width] = dot_nt(scaled[...], grads[...])
    wgrad_ref[:, 3 * width :] = dot_nt(cot_ref[...], context[...])
    whole = jnp.concatenate([weight_ref[i] for i in range(3)], axis=0)
    part = dot_tn(whole, grads[...]).astype(BF16)
    part_ref[...] = part
    weighted = part.astype(F32) * gain
    stats_ref[0:1, :] = jnp.sum(weighted, axis=0, keepdims=True)
    stats_ref[1:2, :] = jnp.sum(weighted * normed[...], axis=0, keepdims=True)
    stats_ref[2:3, :] = inv
    stats_ref[3:8, :] = jnp.zeros((5, rows), F32)
    own = pl.ds(pl.multiple_of(head_ref[0] * width, width), width)
    own_ref[...] = full_ref[own, :]
    normown_ref[...] = normed[own, :]
    gainown_ref[...] = jnp.broadcast_to(gain, (channels, 128))


def return_kernel(
    ns, nh, branch_ref, part_ref, stats_ref, wgrad_ref, own_ref, normown_ref, gain_ref, cot_ref, code_ref,
    mixed_ref, back_ref, wsum_ref, gsum_ref,
    branch_in, part_in, stats_in, wgrad_in, gain_out, gain_in, buckets,
    head_send, head_recv, scan_send, scan_recv,
):
    s, h = lax.axis_index("scan"), lax.axis_index("head")
    width, rows = own_ref.shape
    channels = width * nh
    strip = channels // ns
    barrier, count = greet(ns, nh, True, True)
    pl.semaphore_wait(barrier, count)

    def remote(src, dst, send, recv, to):
        return pltpu.make_async_remote_copy(
            src_ref=src, dst_ref=dst, send_sem=send, recv_sem=recv, device_id=to, device_id_type=MESH
        )

    def head_copy(which, j):
        peer = lax.rem(h + j, nh)
        piece = pl.ds(pl.multiple_of(peer * width, width), width)
        src = (part_ref.at[piece, :], branch_ref.at[piece, :], stats_ref)[which]
        dst = (part_in, branch_in, stats_in)[which].at[h]
        return remote(src, dst, head_send.at[which, j], head_recv.at[which, j], (s, peer))

    def scan_copy(which, j):
        peer = lax.rem(s + j, ns)
        if which == 0:
            src = wgrad_ref.at[pl.ds(pl.multiple_of(peer * strip, strip), strip), :]
            dst = wgrad_in.at[s]
        elif which == 1:
            src, dst = buckets.at[peer], back_ref.at[s]
        else:
            src, dst = gain_out, gain_in.at[s]
        return remote(src, dst, scan_send.at[which, j], scan_recv.at[which, j], (peer, h))

    def each(count, act):
        def body(j, carry):
            act(j)
            return carry

        lax.fori_loop(1, count, body, 0)

    each(nh, lambda j: head_copy(2, j).start())
    each(nh, lambda j: head_copy(0, j).start())
    each(nh, lambda j: head_copy(1, j).start())
    each(ns, lambda j: scan_copy(0, j).start())
    mine = pl.ds(pl.multiple_of(h * width, width), width)
    part_in[pl.ds(h, 1)] = part_ref[mine, :][None]
    branch_in[pl.ds(h, 1)] = branch_ref[mine, :][None]
    stats_in[pl.ds(h, 1)] = stats_ref[...][None]
    wgrad_in[pl.ds(s, 1)] = wgrad_ref[pl.ds(pl.multiple_of(s * strip, strip), strip), :][None]
    each(nh, lambda j: head_copy(2, j).wait())
    each(nh, lambda j: head_copy(0, j).wait())
    normed_grad = part_in[0].astype(F32)
    stats = stats_in[0]
    for i in range(1, nh):
        normed_grad = normed_grad + part_in[i].astype(F32)
        stats = stats + stats_in[i]
    gain = gain_ref[mine, :][:, :1]
    normed = normown_ref[...]
    inv = stats_ref[2:3, :]
    first, second = stats[0:1] * (1.0 / channels), stats[1:2] * (1.0 / channels)
    grad = inv * (normed_grad * gain - first - normed * second)
    points_grad = (cot_ref[...].astype(F32) + grad).astype(BF16)
    code = code_ref[...]
    for i in range(ns // 4):
        block = dot_nt(points_grad, hot_block(code, 512 * i, 512)).astype(BF16)
        for t in range(4):
            buckets[4 * i + t] = block[:, 128 * t : 128 * (t + 1)]
    each(ns, lambda j: scan_copy(1, j).start())
    back_ref[pl.ds(s, 1)] = buckets[pl.ds(s, 1)]
    product = normed_grad * normed
    folded = product[:, :128]
    for b in range(128, rows, 128):
        folded = folded + product[:, b : b + 128]
    gain_row = jnp.sum(jnp.transpose(folded), axis=0, keepdims=True)
    gain_out[...] = jnp.zeros_like(gain_out)
    gain_out[0:1, :width] = gain_row
    each(ns, lambda j: scan_copy(2, j).start())
    gain_in[pl.ds(s, 1)] = gain_out[...][None]
    each(nh, lambda j: head_copy(1, j).wait())
    branch = branch_in[0].astype(F32)
    for i in range(1, nh):
        branch = branch + branch_in[i].astype(F32)
    mixed_ref[...] = (own_ref[...].astype(F32) + branch).astype(BF16)
    each(ns, lambda j: scan_copy(0, j).wait())
    wsum_ref[...] = jnp.sum(wgrad_in[...], axis=0)
    each(ns, lambda j: scan_copy(2, j).wait())
    gsum_ref[...] = jnp.sum(gain_in[...], axis=0)
    each(ns, lambda j: scan_copy(1, j).wait())


def slots_kernel(
    ns, sizes_ref, back_ref, mixed_in, wsum_ref, gsum_ref,
    mixed_ref, owned_ref, qkv_ref, out_ref, gain_ref, slots,
):
    width = back_ref.shape[1]
    slots[...] = jnp.zeros_like(slots)
    lane = lax.broadcasted_iota(jnp.int32, (width, 128), 1)

    def one(d, begin):
        size = sizes_ref[d, 0]
        tile = begin // 128
        off = begin - tile * 128
        block = jnp.where(lane < size, back_ref[d].astype(F32), 0.0)
        wide = jnp.concatenate([block, jnp.zeros_like(block)], axis=1)
        at = pl.ds(pl.multiple_of(tile * 128, 128), 256)
        slots[:, at] = slots[:, at] + pltpu.roll(wide, off, 1)
        return begin + size

    lax.fori_loop(0, ns, one, jnp.int32(0))
    owned_ref[...] = slots[...].astype(BF16)
    mixed_ref[...] = mixed_in[...]
    turned = jnp.transpose(wsum_ref[...])
    for i in range(3):
        qkv_ref[i] = turned[i * width : (i + 1) * width]
    out_ref[...] = turned[3 * width :]
    gain_ref[...] = gsum_ref[0:1, :width]


def per_device(owner_ids, owned_points, norm_gain, qkv_weight, out_weight, cotangent):
    ns, nh = lax.axis_size("scan"), lax.axis_size("head")
    rows = owner_ids.shape[0]
    width, slot_count = owned_points.shape
    channels = width * nh
    strip = channels // ns
    shape = jax.ShapeDtypeStruct
    dma = pltpu.SemaphoreType.DMA

    def remote_params(number):
        return pltpu.CompilerParams(
            collective_id=number, has_side_effects=True, vmem_limit_bytes=LIMIT
        )

    local_params = pltpu.CompilerParams(vmem_limit_bytes=LIMIT)
    code, sizes = pl.pallas_call(
        functools.partial(tally_kernel, ns),
        out_shape=(shape((1, rows), jnp.int32), shape((ns, 128), jnp.int32)),
        in_specs=[VMEM],
        out_specs=(VMEM, VMEM),
        scratch_shapes=[pltpu.VMEM((ns, 128), jnp.int32), dma((ns,)), dma((ns,))],
        compiler_params=remote_params(1),
        name="tally",
    )(owner_ids.reshape(1, rows))
    send_rows = pl.pallas_call(
        functools.partial(window_kernel, ns),
        out_shape=shape((ns, width, BUCKET), BF16),
        in_specs=[SMEM, VMEM],
        out_specs=VMEM,
        compiler_params=local_params,
        name="windows",
    )(sizes, owned_points)
    full, cot_full = pl.pallas_call(
        functools.partial(gather_kernel, ns, nh),
        out_shape=(shape((channels, rows), BF16), shape((channels, rows), BF16)),
        in_specs=[VMEM] * 3,
        out_specs=(VMEM, VMEM),
        scratch_shapes=[
            pltpu.VMEM((ns, width, BUCKET), BF16),
            pltpu.VMEM((ns * BUCKET, rows), BF16),
            dma((ns,)),
            dma((ns,)),
            dma((2, nh)),
            dma((2, nh)),
        ],
        compiler_params=remote_params(2),
        name="gather_points",
    )(send_rows, code, cotangent)
    branch, part, stats, wgrad, own, normown, gain_wide = pl.pallas_call(
        block_kernel,
        out_shape=(
            shape((channels, rows), BF16),
            shape((channels, rows), BF16),
            shape((8, rows), F32),
            shape((channels, 4 * width), F32),
            shape((width, rows), BF16),
            shape((width, rows), F32),
            shape((channels, 128), F32),
        ),
        in_specs=[VMEM] * 5 + [SMEM],
        out_specs=(VMEM,) * 7,
        scratch_shapes=[
            pltpu.VMEM((channels, rows), F32),
            pltpu.VMEM((channels, rows), BF16),
            pltpu.VMEM((width, rows), F32),
            pltpu.VMEM((width, rows), F32),
            pltpu.VMEM((width, rows), F32),
            pltpu.VMEM((width, rows), F32),
            pltpu.VMEM((width, rows), BF16),
            pltpu.VMEM((3 * width, rows), BF16),
            pltpu.VMEM((rows, 6 * HD), BF16),
            pltpu.VMEM((rows, 7 * HD), BF16),
        ],
        compiler_params=local_params,
        name="attention_block",
    )(
        full, cot_full, norm_gain.reshape(1, channels), qkv_weight, out_weight,
        lax.axis_index("head").astype(jnp.int32).reshape(1),
    )
    mixed, back, wsum, gsum = pl.pallas_call(
        functools.partial(return_kernel, ns, nh),
        out_shape=(
            shape((width, rows), BF16),
            shape((ns, width, BUCKET), BF16),
            shape((strip, 4 * width), F32),
            shape((8, 128), F32),
        ),
        in_specs=[VMEM] * 9,
        out_specs=(VMEM,) * 4,
        scratch_shapes=[
            pltpu.VMEM((nh, width, rows), BF16),
            pltpu.VMEM((nh, width, rows), BF16),
            pltpu.VMEM((nh, 8, rows), F32),
            pltpu.VMEM((ns, strip, 4 * width), F32),
            pltpu.VMEM((8, 128), F32),
            pltpu.VMEM((ns, 8, 128), F32),
            pltpu.VMEM((ns, width, BUCKET), BF16),
            dma((3, nh)),
            dma((3, nh)),
            dma((3, ns)),
            dma((3, ns)),
        ],
        compiler_params=remote_params(3),
        name="return_points",
    )(branch, part, stats, wgrad, own, normown, gain_wide, cotangent, code)
    mixed_rows, grad_owned, qkv_grad, out_grad, gain_grad = pl.pallas_call(
        functools.partial(slots_kernel, ns),
        out_shape=(
            shape((width, rows), BF16),
            shape((width, slot_count), BF16),
            shape((3, width, strip), F32),
            shape((width, strip), F32),
            shape((1, width), F32),
        ),
        in_specs=[SMEM] + [VMEM] * 4,
        out_specs=(VMEM,) * 5,
        scratch_shapes=[pltpu.VMEM((width, slot_count), F32)],
        compiler_params=local_params,
        name="slots",
    )(sizes, back, mixed, wsum, gsum)
    return mixed_rows, grad_owned, qkv_grad, out_grad, gain_grad.reshape(width)


def solution(mesh):
    in_specs = (
        P("scan", None),
        P("head", "scan"),
        P(),
        P(None, "head", None),
        P("head", None),
        P("head", "scan"),
    )
    out_specs = (
        P("head", "scan"),
        P("head", "scan"),
        P(None, "head", "scan"),
        P("head", "scan"),
        P("head"),
    )
    return jax.shard_map(
        per_device, mesh=mesh, in_specs=in_specs, out_specs=out_specs, check_vma=False
    )
```

time: 834 us -> 136 us (0.16); the launches traced: 821 us -> 136 us
  waiting for transfers between devices: 431 us -> 0 us
  Pallas kernels: 0 us -> 132 us
  local copies, waits for them, and re-layouts: 119 us -> 3.01 us
  matrix products: 112 us -> 0 us
  blocking collectives: 80.8 us -> 0 us
  other arithmetic: 32.2 us -> 0 us
  starting transfers between devices: 22 us -> 0 us
  between operations: 15.5 us -> 0.66 us
  loops' own time: 9.42 us -> 0 us
    reduce_scatter x2 -> x0, waiting for transfers between devices: 362 us -> none  [the longest x1 218 us: per_device(): lax.psum_scatter(qkv_grad_local, 'scan', scatter_dimension=2, tiled=True)]
    pallas_call x0 -> x6, Pallas kernels: none -> 132 us  [the longest x1 47.1 us: per_device(): pl.pallas_call(functools.partial(return_kernel, ns, nh), out_shape=(shape...]
    dot_general x62 -> x0, matrix products: 112 us -> none  [the longest x8 18.6 us: attend_back(): jnp.einsum('dq,dk->qk', chosen_grad, values, precision=PRECISE)]
    gather x97 -> x0, local copies, waits for them, and re-layouts: 91.5 us -> none
    psum x1 -> x0, blocking collectives: 60.8 us -> none  [per_device(): gain_grad = lax.psum(jnp.sum(normed_grad * normed_local, axis=1), 'scan')]
    psum x1 -> x0, waiting for transfers between devices: 24.6 us -> none  [per_device(): lax.psum(partial_input.astype(jnp.bfloat16), 'head').astype(jnp.float32)]
    all_gather x2 -> x0, waiting for transfers between devices: 22.6 us -> none  [the longest x1 22.6 us: per_device(): full_rows = lax.all_gather(regrouped, 'head', axis=0, tiled=True)]
    all_to_all x4 -> x0, starting transfers between devices: 21.7 us -> none  [the longest x1 9.7 us: per_device(): lax.all_to_all(send_back, 'scan', split_axis=0, concat_axis=0, tiled=True)]
  transfers between devices with their start and end apart: 10 -> 0, of which waited for: 6 -> 0; matrix products, arithmetic and copies ran while one was open for 30% -> 0% of each run, Pallas kernels for 0% -> 0%
where the time goes in v1:
time: 136 us
  Pallas kernels  132 us (97%)
  local copies, waits for them, and re-layouts  3.01 us (2%)
    pallas_call x1, Pallas kernels, per_device(): pl.pallas_call(functools.partial(return_kernel, ns, nh), out_shape=(shape...  47.1 us
    pallas_call x1, Pallas kernels, per_device(): pl.pallas_call(functools.partial(gather_kernel, ns, nh), out_shape=(shape...  32.5 us
    pallas_call x1, Pallas kernels, per_device(): pl.pallas_call(block_kernel, out_shape=(shape((channels, rows), BF16), sh...  27.4 us
    pallas_call x1, Pallas kernels, per_device(): pl.pallas_call(functools.partial(tally_kernel, ns), out_shape=(shape((1,...  15.7 us
    pallas_call x1, Pallas kernels, per_device(): pl.pallas_call(functools.partial(slots_kernel, ns), out_shape=(shape((wid...  4.94 us
    pallas_call x1, Pallas kernels, per_device(): pl.pallas_call(functools.partial(window_kernel, ns), out_shape=shape((ns,...  4.54 us
    unnamed x2, local copies, waits for them, and re-layouts  3.01 us

profile of v1, /device:TPU:1, one launch (start us, length us, event | category | flops | bytes accessed | tf_op | source)
XLA Modules:
  0.0 135.8 jit_solution(12959692164541865689)
XLA Ops:
  0.6 15.7 %tally.1 = (s32[1,1024]{1,0:T(1,128)}, s32[32,128]{1,0:T(8,128)}) custom-call(s32[1,1024]{1,0:T(1,128)} %bitcast.4), custom_call_target="tpu_custom_call" | custom-call | tf_op jit(solution)/shard_map/tally/pallas_call | solution.py:451
  16.4 4.5 %windows.1.send_ref = bf16[32,64,128]{2,1,0:T(8,128)(2,1)} custom-call(s32[32,128]{1,0:T(8,128)} %get-tuple-element.25.sizes_ref, bf16[64,4224]{1,0:T(8,128)(2,1)} %points_ref.1), custom_call_target="tpu_custom_call" | custom-call | tf_op jit(solution)/shard_map/windows/pallas_call | solution.py:460
  20.9 32.5 %gather_points.1 = (bf16[512,1024]{1,0:T(8,128)(2,1)}, bf16[512,1024]{1,0:T(8,128)(2,1)}) custom-call(bf16[32,64,128]{2,1,0:T(8,128)(2,1)} %windows.1.send_ref, s32[1,1024]{1,0:T(1,128)} %get-tuple-element.26.code_ref, bf16[64,1024]{1,0:T(8,128)(2,1)} %cot_ref.3), custom_call_target="tpu_custom_call" | custom-call | tf_op jit(solution)/shard_map/gather_points/pallas_call | solution.py:468
  53.4 27.4 %attention_block.1 = (bf16[512,1024]{1,0:T(8,128)(2,1)}, bf16[512,1024]{1,0:T(8,128)(2,1)}, f32[8,1024]{1,0:T(8,128)}, f32[512,256]{1,0:T(8,128)}, bf16[64,1024]...) custom-call(bf16[512,1024]{1,0:T(8,128)(2,1)} %get-tuple-element.27.full_ref, ...), custom_call_target="tpu_custom_call" | custom-call | tf_op jit(solution)/shard_map/attention_block/pallas_call | solution.py:484
  80.8 47.1 %return_points.1 = (bf16[64,1024]{1,0:T(8,128)(2,1)}, bf16[32,64,128]{2,1,0:T(8,128)(2,1)}, f32[16,256]{1,0:T(8,128)}, f32[8,128]{1,0:T(8,128)}) custom-call(bf16[512,1024]{1,0:T(8,128)(2,1)} %get-tuple-element.29.branch_ref, bf16[512,1024]{1,0:T(8,128)(2,1)} %get-tuple-element.30.part_ref, f32[8,1024]{1,0:T(8,128)} %get-tuple-element.31.stats_ref, ...), custom_call_target="tpu_custom_call" | custom-call | tf_op jit(solution)/shard_map/return_points/pallas_call | solution.py:515
  127.9 4.9 %slots.1 = (bf16[64,1024]{1,0:T(8,128)(2,1)}, bf16[64,4224]{1,0:T(8,128)(2,1)}, f32[3,64,16]{2,1,0:T(8,128)}, f32[64,16]{1,0:T(8,128)}, f32[1,64]{1,0:T(1,128)}) custom-call(s32[32,128]{1,0:T(8,128)} %get-tuple-element.25.sizes_ref, bf16[32,64,128]{2,1,0:T(8,128)(2,1)} %get-tuple-element.36.back_ref, bf16[64,1024]{1,0:T(8,128)(2,1)} %get-tuple-element.37.mixed_in, ...), custom_call_target="tpu_custom_call" | custom-call | tf_op jit(solution)/shard_map/slots/pallas_call | solution.py:541
  132.8 1.4 %copy.12 = f32[64,16]{0,1:T(8,128)} copy(f32[64,16]{1,0:T(8,128)} %get-tuple-element.48) | data formatting | bytes 8192
  134.2 1.6 %copy.11 = f32[3,64,16]{1,2,0:T(8,128)} copy(f32[3,64,16]{2,1,0:T(8,128)} %get-tuple-element.47) | data formatting | bytes 24576

commit v2 on v0

v2 whole, which is shorter than its diff:
```python
import functools

import jax
import jax.numpy as jnp
from jax import lax
from jax.experimental import pallas as pl
from jax.experimental.pallas import tpu as pltpu
from jax.sharding import PartitionSpec as P

HD = 16
BUCKET = 128
EPS = 1e-05
SPAN = 256
LOG2E = 1.4426950408889634
MESH = pl.DeviceIdType.MESH
F32 = jnp.float32
BF16 = jnp.bfloat16
VMEM = pl.BlockSpec(memory_space=pltpu.VMEM)
SMEM = pl.BlockSpec(memory_space=pltpu.SMEM)
LIMIT = 56 * 1024 * 1024


def dot_nn(a, b):
    return lax.dot_general(a, b, (((1,), (0,)), ((), ())), preferred_element_type=F32)


def dot_nt(a, b):
    return lax.dot_general(a, b, (((1,), (1,)), ((), ())), preferred_element_type=F32)


def dot_tn(a, b):
    return lax.dot_general(a, b, (((0,), (0,)), ((), ())), preferred_element_type=F32)


def split2(x):
    high = x.astype(BF16)
    return high, (x - high.astype(F32)).astype(BF16)


def split3(x):
    high = x.astype(BF16)
    rest = x - high.astype(F32)
    middle = rest.astype(BF16)
    return high, middle, (rest - middle.astype(F32)).astype(BF16)


def left_stack(x):
    a, b, c = split3(x)
    return [a, b, a, b, c, a]


def right_stack(x):
    a, b, c = split3(x)
    return [a, a, b, b, a, c]


def hot_block(code, first, height):
    ids = lax.broadcasted_iota(jnp.int32, (height, code.shape[1]), 0) + first
    return jnp.where(ids == code, 1.0, 0.0).astype(BF16)


def aligned(first, size):
    return pl.ds(pl.multiple_of(first, size), size)


def each(first, last, act):
    def body(j, carry):
        act(j)
        return carry

    lax.fori_loop(first, last, body, 0)


TALLY, POINTS, WGRAD, BACK, GAIN = range(5)
COT, FULL, BRANCH, STATS, TWIN, PAIR = range(6)


def main_kernel(
    ns, nh, owner_ref, points_ref, cot_ref, gain_ref, weight_ref, outw_ref,
    sizes_ref, mixed_ref, back_ref, wsum_ref, gsum_ref,
    tall, tiles, offsets, windows, arrived, hots, full, cot, code_ref, gain_wide,
    normed, scaled, query, keys, value, gradc, context, grads, weights_all, shares,
    key_t, value_t, branch_out, branch_in, part_out, twin_in, pair_out, pair_in, stats_out, stats_in,
    wgrad_out, wgrad_in, gain_out, gain_in, buckets,
    scan_send, scan_recv, head_send, head_recv,
):
    s, h = lax.axis_index("scan"), lax.axis_index("head")
    nx = nh // 2
    x, core = h // 2, lax.rem(h, 2)
    twin = x * 2 + 1 - core
    width, rows = cot_ref.shape
    channels = width * nh
    strip = channels // ns
    mine = aligned(h * width, width)

    def remote(src, dst, send, recv, to):
        return pltpu.make_async_remote_copy(
            src_ref=src, dst_ref=dst, send_sem=send, recv_sem=recv, device_id=to, device_id_type=MESH
        )

    def scan_copy(which, j):
        peer = lax.rem(s + j, ns)
        if which == TALLY:
            src, dst = tall.at[pl.ds(peer, 1), :], sizes_ref.at[pl.ds(s, 1), :]
        elif which == POINTS:
            src, dst = windows.at[peer], arrived.at[s]
        elif which == WGRAD:
            src, dst = wgrad_out.at[aligned(peer * strip, strip), :], wgrad_in.at[s]
        elif which == BACK:
            src, dst = buckets.at[peer], back_ref.at[s]
        else:
            src, dst = gain_out, gain_in.at[s]
        return remote(src, dst, scan_send.at[which, j], scan_recv.at[which, j], (peer, h))

    def head_copy(which, j):
        peer = lax.rem(h + j, nh)
        if which == BRANCH:
            src, dst = branch_out.at[aligned(peer * width, width), :], branch_in.at[h]
        else:
            src, dst = stats_out, stats_in.at[h]
        return remote(src, dst, head_send.at[which, j], head_recv.at[which, j], (s, peer))

    def push(which, ref, piece, slot, to):
        block = ref.at[aligned(piece * width, width), :]
        return remote(block, block, head_send.at[which, slot], head_recv.at[which, piece], (s, to))

    def spread(which, ref):
        for j in (nx // 2, *[j for j in range(1, nx) if j != nx // 2]):
            push(which, ref, h, j, lax.rem(x + j, nx) * 2 + core).start()
        push(which, ref, h, 0, twin).start()

    def relay(which, ref):
        for j in range(1, nx):
            piece = lax.rem(x + nx - j, nx) * 2 + core
            push(which, ref, piece, nx + j, twin).wait_recv()
            push(which, ref, piece, nx + j, twin).start()

    def arrive(which, ref):
        for j in range(nx):
            piece = lax.rem(x + nx - j, nx) * 2 + 1 - core
            push(which, ref, piece, 0, twin).wait_recv()

    def sent(which, ref):
        for j in range(1, nx):
            push(which, ref, h, j, twin).wait_send()
            push(which, ref, h, nx + j, twin).wait_send()
        push(which, ref, h, 0, twin).wait_send()

    barrier = pltpu.get_barrier_semaphore()

    def greet_scan(j):
        pl.semaphore_signal(
            barrier, inc=1, device_id=(lax.rem(s + j, ns), h), device_id_type=MESH
        )

    def greet_head(j):
        pl.semaphore_signal(
            barrier, inc=1, device_id=(s, lax.rem(h + j, nh)), device_id_type=MESH
        )

    each(1, ns, greet_scan)
    each(1, nh, greet_head)
    owners = owner_ref[...]
    hot = lax.broadcasted_iota(jnp.int32, (ns, rows), 0) == owners
    ones = jnp.where(hot, 1.0, 0.0)
    total = jnp.sum(jnp.where(hot, 1, 0), axis=1, keepdims=True)
    tall[...] = jnp.broadcast_to(total, (ns, 128))
    cot[mine, :] = cot_ref[...]
    pl.semaphore_wait(barrier, ns + nh - 2)

    each(1, ns, lambda j: scan_copy(TALLY, j).start())
    spread(COT, cot)
    sizes_ref[pl.ds(s, 1), :] = tall[pl.ds(s, 1), :]
    before = jnp.where(
        lax.broadcasted_iota(jnp.int32, (128, 128), 0)
        < lax.broadcasted_iota(jnp.int32, (128, 128), 1),
        1.0,
        0.0,
    ).astype(BF16)
    carried = jnp.zeros((ns, 1), F32)
    for b in range(0, rows, 128):
        part = ones[:, b : b + 128]
        running = dot_nn(part.astype(BF16), before) + carried
        rank = jnp.sum(running * part, axis=0, keepdims=True)
        code_ref[:, b : b + 128] = owners[:, b : b + 128] * BUCKET + rank.astype(jnp.int32)
        carried = carried + jnp.sum(part, axis=1, keepdims=True)
    each(1, ns, lambda j: scan_copy(TALLY, j).wait())

    earlier = jnp.where(
        lax.broadcasted_iota(jnp.int32, (ns, ns), 1) < lax.broadcasted_iota(jnp.int32, (ns, ns), 0),
        1.0,
        0.0,
    ).astype(BF16)
    begins = dot_nn(earlier, sizes_ref[...].astype(F32).astype(BF16)).astype(jnp.int32)
    tiles[...] = begins // 128
    offsets[...] = begins - begins // 128 * 128
    span = lax.broadcasted_iota(jnp.int32, (256, 128), 0) - lax.broadcasted_iota(
        jnp.int32, (256, 128), 1
    )
    groups = ns // 4

    def nth_group(i):
        half = (i + 1) // 2
        shift = groups // 2 + jnp.where(lax.rem(i, 2) == 1, half, -half)
        return lax.rem(s // 4 + shift + groups, groups)

    def cut_and_send(i):
        group = nth_group(i)
        places = [jnp.broadcast_to(tiles[pl.ds(group * 4 + t, 1), :], (16, 128)) for t in range(4)]
        low = [jnp.zeros((width // 16, 16, 128), BF16) for t in range(4)]
        high = [jnp.zeros((width // 16, 16, 128), BF16) for t in range(4)]
        previous = [jnp.zeros((1, 16, 128), BF16) for t in range(4)]
        for n in range(ns + 1):
            tile = points_ref[:, 128 * n : 128 * (n + 1)].reshape(width // 16, 16, 128)
            for t in range(4):
                here = jnp.where(places[t] == n, 1.0, 0.0).astype(BF16)[None]
                high[t] = high[t] + tile * previous[t]
                if n < ns:
                    low[t] = low[t] + tile * here
                previous[t] = here
        for t in range(4):
            peer = group * 4 + t
            window = jnp.concatenate(
                [low[t].reshape(width, 128), high[t].reshape(width, 128)], axis=1
            )
            pick = jnp.where(span == offsets[pl.ds(peer, 1), :], 1.0, 0.0).astype(BF16)
            windows[peer] = dot_nn(window, pick).astype(BF16)

            @pl.when(peer != s)
            def _():
                scan_copy(POINTS, lax.rem(peer - s + ns, ns)).start()

    each(0, groups, cut_and_send)
    arrived[pl.ds(s, 1)] = windows[pl.ds(s, 1)]
    code = code_ref[...]

    def build(i):
        first = pl.multiple_of(i * 256, 256)
        hots[pl.ds(first, 256), :] = hot_block(code, first, 256)

    each(0, ns // 2, build)
    relay(COT, cot)
    gain = jnp.transpose(jnp.broadcast_to(gain_ref[...], (8, channels)))[:, :1]
    gain_wide[...] = jnp.broadcast_to(gain, gain_wide.shape)
    arrive(COT, cot)
    gradc[...] = dot_nn(outw_ref[...], cot[...])

    gathered = jnp.zeros((width, rows), F32)
    for i in range(groups):
        group = nth_group(i)
        for t in range(4):
            source = group * 4 + t

            @pl.when(source != s)
            def _():
                scan_copy(POINTS, lax.rem(s - source + ns, ns)).wait_recv()

        pieces = jnp.concatenate([arrived[group * 4 + t] for t in range(4)], axis=1)
        gathered = gathered + dot_nn(pieces, hots[aligned(group * 512, 512), :])
    full[mine, :] = gathered.astype(BF16)
    spread(FULL, full)
    relay(FULL, full)
    arrive(FULL, full)

    floats = full[...].astype(F32)
    mean = jnp.sum(floats, axis=0, keepdims=True) * (1.0 / channels)
    centered = floats - mean
    inv = lax.rsqrt(jnp.sum(centered * centered, axis=0, keepdims=True) * (1.0 / channels) + EPS)
    normed[...] = centered * inv
    scaled[...] = (normed[...] * gain_wide[:, :1]).astype(BF16)
    for i, ref in enumerate((query, keys, value)):
        ref[...] = dot_nn(weight_ref[i], scaled[...])

    def forward(head):
        at = aligned(head * HD, HD)
        q, k, v = query[at, :], keys[at, :], value[at, :]
        key_t[...] = jnp.transpose(jnp.concatenate(left_stack(k), axis=0))
        v_rows = jnp.concatenate(list(split2(v)) + [jnp.ones((HD, rows), BF16)], axis=0)
        for b in range(0, rows, SPAN):
            q_stack = jnp.concatenate(
                right_stack(q[:, b : b + SPAN] * (HD**-0.5 * LOG2E)), axis=0
            )
            scores = dot_nn(key_t[...], q_stack)
            peak = jnp.max(scores, axis=0, keepdims=True)
            weights = jnp.exp2(scores - peak).astype(BF16)
            weights_all[head, :, b : b + SPAN] = weights
            sums = dot_nn(v_rows, weights)
            share = 1.0 / sums[2 * HD : 2 * HD + 1]
            shares[head, :, b : b + SPAN] = share
            ctx = (sums[:HD] + sums[HD : 2 * HD]) * share
            context[at, b : b + SPAN] = ctx

    each(0, width // HD, forward)
    context_b = context[...].astype(BF16)
    branch_out[...] = dot_tn(outw_ref[...], context_b).astype(BF16)
    each(1, nh, lambda j: head_copy(BRANCH, j).start())

    def backward(head):
        at = aligned(head * HD, HD)
        q, k, v = query[at, :], keys[at, :], value[at, :]
        row = lax.broadcasted_iota(jnp.int32, (HD, rows), 0)
        ones = jnp.ones((HD, rows), BF16)
        value_t[...] = jnp.transpose(jnp.concatenate(left_stack(v) + [ones], axis=0))
        k_rows = jnp.concatenate(list(split2(k)), axis=0)
        gs = gradc[at, :] * shares[head]
        center = jnp.sum(gs * context[at, :], axis=0, keepdims=True) * (-(HD**-0.5))
        parts = [t.astype(F32) for t in split3(center)]
        tail = jnp.where(
            row == 0, parts[0], jnp.where(row == 1, parts[1], jnp.where(row == 2, parts[2], 0.0))
        ).astype(BF16)
        g_stack = jnp.concatenate(right_stack(gs * HD**-0.5) + [tail], axis=0)
        g_rows = jnp.concatenate(list(split2(gs)), axis=0)
        q_rows = jnp.concatenate(list(split2(q)), axis=0)
        key_grad = jnp.zeros((HD * 2, rows), F32)
        value_grad = jnp.zeros((HD * 2, rows), F32)
        for b in range(0, rows, SPAN):
            weights = weights_all[head, :, b : b + SPAN]
            delta = dot_nn(value_t[...], g_stack[:, b : b + SPAN])
            score_grad = (weights.astype(F32) * delta).astype(BF16)
            value_grad = value_grad + dot_nt(g_rows[:, b : b + SPAN], weights)
            dq = dot_nn(k_rows, score_grad)
            grads[at, b : b + SPAN] = (dq[:HD] + dq[HD:]).astype(BF16)
            key_grad = key_grad + dot_nt(q_rows[:, b : b + SPAN], score_grad)
        k_at = aligned(width + head * HD, HD)
        v_at = aligned(2 * width + head * HD, HD)
        grads[k_at, :] = (key_grad[:HD] + key_grad[HD:]).astype(BF16)
        grads[v_at, :] = (value_grad[:HD] + value_grad[HD:]).astype(BF16)

    each(0, width // HD, backward)

    whole = jnp.concatenate([weight_ref[i] for i in range(3)], axis=0)
    part_out[...] = dot_tn(whole, grads[...]).astype(BF16)

    def twin_copy(j):
        to = lax.rem(x + j, nx)
        src = part_out.at[aligned((to * 2 + 1 - core) * width, width), :]
        return remote(src, twin_in.at[j], head_send.at[TWIN, j], head_recv.at[TWIN, j], (s, twin))

    def pair_copy(j):
        to = lax.rem(x + j, nx) * 2 + core
        return remote(
            pair_out.at[j], pair_in.at[j], head_send.at[PAIR, j], head_recv.at[PAIR, j], (s, to)
        )

    order = (*([nx // 2] if nx > 1 else []), *[j for j in range(1, nx) if j != nx // 2])
    for j in (*order, 0):
        twin_copy(j).start()
    weighted = part_out[...].astype(F32) * gain_wide[:, :1]
    stats_out[0:1, :] = jnp.sum(weighted, axis=0, keepdims=True)
    stats_out[1:2, :] = jnp.sum(weighted * normed[...], axis=0, keepdims=True)
    each(1, nh, lambda j: head_copy(STATS, j).start())

    def pair_sum(j):
        twin_copy(j).wait_recv()
        own = part_out[aligned((lax.rem(x + j, nx) * 2 + core) * width, width), :]
        return own.astype(F32) + twin_in[j].astype(F32)

    for j in order:
        pair_out[j] = pair_sum(j).astype(BF16)
        pair_copy(j).start()
    normed_grad = pair_sum(0)
    wgrad_out[:, : 3 * width] = dot_nt(scaled[...], grads[...]).astype(BF16)
    wgrad_out[:, 3 * width :] = dot_nt(cot[...], context_b).astype(BF16)
    each(1, ns, lambda j: scan_copy(WGRAD, j).start())
    wgrad_in[pl.ds(s, 1)] = wgrad_out[aligned(s * strip, strip), :][None]
    each(1, nh, lambda j: head_copy(BRANCH, j).wait())
    branch = branch_out[mine, :].astype(F32)
    for i in range(1, nh):
        branch = branch + branch_in[lax.rem(h + i, nh)].astype(F32)
    mixed_ref[...] = (full[mine, :].astype(F32) + branch).astype(BF16)
    each(1, nh, lambda j: head_copy(STATS, j).wait())
    stats = stats_out[...]
    for i in range(1, nh):
        stats = stats + stats_in[lax.rem(h + i, nh)]
    for j in order:
        pair_copy(j).wait_recv()
        normed_grad = normed_grad + pair_in[j].astype(F32)
    normed_own = normed[mine, :]
    first, second = stats[0:1] * (1.0 / channels), stats[1:2] * (1.0 / channels)
    grad = inv * (normed_grad * gain_wide[mine, :1] - first - normed_own * second)
    points_grad = (cot_ref[...].astype(F32) + grad).astype(BF16)

    for i in range(groups):
        group = nth_group(i)
        block = dot_nt(points_grad, hots[aligned(group * 512, 512), :]).astype(BF16)
        for t in range(4):
            peer = group * 4 + t
            buckets[peer] = block[:, 128 * t : 128 * (t + 1)]

            @pl.when(peer != s)
            def _():
                scan_copy(BACK, lax.rem(peer - s + ns, ns)).start()

    back_ref[pl.ds(s, 1)] = buckets[pl.ds(s, 1)]
    product = normed_grad * normed_own
    folded = product[:, :128]
    for b in range(128, rows, 128):
        folded = folded + product[:, b : b + 128]
    gain_out[...] = jnp.zeros_like(gain_out)
    gain_out[:, :width] = jnp.sum(jnp.transpose(folded), axis=0, keepdims=True)
    each(1, ns, lambda j: scan_copy(GAIN, j).start())
    gain_in[pl.ds(s, 1)] = gain_out[...][None]
    each(1, ns, lambda j: scan_copy(WGRAD, j).wait())
    wsum_ref[...] = jnp.sum(wgrad_in[...].astype(F32), axis=0)
    each(1, ns, lambda j: scan_copy(GAIN, j).wait())
    gsum_ref[...] = jnp.sum(gain_in[...], axis=0)
    sent(COT, cot)
    sent(FULL, full)
    for j in (*order, 0):
        twin_copy(j).wait_send()
    for j in order:
        pair_copy(j).wait_send()
    each(1, ns, lambda j: scan_copy(POINTS, j).wait_send())
    each(1, ns, lambda j: scan_copy(BACK, j).wait())


def slots_kernel(
    ns, sizes_ref, back_ref, mixed_in, wsum_ref, gsum_ref,
    mixed_ref, owned_ref, qkv_ref, out_ref, gain_ref, slots,
):
    width = back_ref.shape[1]
    slots[...] = jnp.zeros_like(slots)
    lane = lax.broadcasted_iota(jnp.int32, (width, 128), 1)

    def one(d, begin):
        size = sizes_ref[d, 0]
        tile = begin // 128
        off = begin - tile * 128
        block = jnp.where(lane < size, back_ref[d].astype(F32), 0.0)
        wide = jnp.concatenate([block, jnp.zeros_like(block)], axis=1)
        at = pl.ds(pl.multiple_of(tile * 128, 128), 256)
        slots[:, at] = slots[:, at] + pltpu.roll(wide, off, 1)
        return begin + size

    lax.fori_loop(0, ns, one, jnp.int32(0))
    owned_ref[...] = slots[...].astype(BF16)
    mixed_ref[...] = mixed_in[...]
    for i in range(3):
        qkv_ref[i] = wsum_ref[:, i * width : (i + 1) * width]
    out_ref[...] = wsum_ref[:, 3 * width :]
    gain_ref[...] = gsum_ref[:, :width]


def per_device(owner_ids, owned_points, norm_gain, qkv_weight, out_weight, cotangent):
    ns, nh = lax.axis_size("scan"), lax.axis_size("head")
    nx = nh // 2
    rows = owner_ids.shape[0]
    width, slot_count = owned_points.shape
    channels = width * nh
    strip = channels // ns
    shape = jax.ShapeDtypeStruct
    dma = pltpu.SemaphoreType.DMA
    vmem = pltpu.VMEM
    sizes, mixed, back, wsum, gsum = pl.pallas_call(
        functools.partial(main_kernel, ns, nh),
        out_shape=(
            shape((ns, 128), jnp.int32),
            shape((width, rows), BF16),
            shape((ns, width, BUCKET), BF16),
            shape((strip, 4 * width), F32),
            shape((1, 128), F32),
        ),
        in_specs=[VMEM] * 6,
        out_specs=(VMEM,) * 5,
        scratch_shapes=[
            vmem((ns, 128), jnp.int32),
            vmem((ns, 128), jnp.int32),
            vmem((ns, 128), jnp.int32),
            vmem((ns, width, BUCKET), BF16),
            vmem((ns, width, BUCKET), BF16),
            vmem((ns * BUCKET, rows), BF16),
            vmem((channels, rows), BF16),
            vmem((channels, rows), BF16),
            vmem((1, rows), jnp.int32),
            vmem((channels, 128), F32),
            vmem((channels, rows), F32),
            vmem((channels, rows), BF16),
            vmem((width, rows), F32),
            vmem((width, rows), F32),
            vmem((width, rows), F32),
            vmem((width, rows), F32),
            vmem((width, rows), F32),
            vmem((3 * width, rows), BF16),
            vmem((width // HD, rows, rows), BF16),
            vmem((width // HD, 1, rows), F32),
            vmem((rows, 6 * HD), BF16),
            vmem((rows, 7 * HD), BF16),
            vmem((channels, rows), BF16),
            vmem((nh, width, rows), BF16),
            vmem((channels, rows), BF16),
            vmem((nx, width, rows), BF16),
            vmem((nx, width, rows), BF16),
            vmem((nx, width, rows), BF16),
            vmem((2, rows), F32),
            vmem((nh, 2, rows), F32),
            vmem((channels, 4 * width), BF16),
            vmem((ns, strip, 4 * width), BF16),
            vmem((1, 128), F32),
            vmem((ns, 1, 128), F32),
            vmem((ns, width, BUCKET), BF16),
            dma((5, ns)),
            dma((5, ns)),
            dma((6, nh)),
            dma((6, nh)),
        ],
        compiler_params=pltpu.CompilerParams(
            collective_id=1, has_side_effects=True, vmem_limit_bytes=LIMIT
        ),
        name="patch_block",
    )(owner_ids.reshape(1, rows), owned_points, cotangent, norm_gain.reshape(1, channels), qkv_weight, out_weight)
    mixed_rows, grad_owned, qkv_grad, out_grad, gain_grad = pl.pallas_call(
        functools.partial(slots_kernel, ns),
        out_shape=(
            shape((width, rows), BF16),
            shape((width, slot_count), BF16),
            shape((3, strip, width), F32),
            shape((strip, width), F32),
            shape((1, width), F32),
        ),
        in_specs=[SMEM] + [VMEM] * 4,
        out_specs=(VMEM,) * 5,
        scratch_shapes=[vmem((width, slot_count), F32)],
        compiler_params=pltpu.CompilerParams(vmem_limit_bytes=LIMIT),
        name="slots",
    )(sizes, back, mixed, wsum, gsum)
    return (
        mixed_rows,
        grad_owned,
        qkv_grad.transpose(0, 2, 1),
        out_grad.T,
        gain_grad.reshape(width),
    )


def solution(mesh):
    in_specs = (
        P("scan", None),
        P("head", "scan"),
        P(),
        P(None, "head", None),
        P("head", None),
        P("head", "scan"),
    )
    out_specs = (
        P("head", "scan"),
        P("head", "scan"),
        P(None, "head", "scan"),
        P("head", "scan"),
        P("head"),
    )
    return jax.shard_map(
        per_device, mesh=mesh, in_specs=in_specs, out_specs=out_specs, check_vma=False
    )
```

time: 834 us -> 104 us (0.12); the launches traced: 821 us -> 104 us
  waiting for transfers between devices: 431 us -> 0 us
  local copies, waits for them, and re-layouts: 119 us -> 0 us
  matrix products: 112 us -> 0 us
  Pallas kernels: 0 us -> 103 us
  blocking collectives: 80.8 us -> 0 us
  other arithmetic: 32.2 us -> 0 us
  starting transfers between devices: 22 us -> 0 us
  between operations: 15.5 us -> 0.64 us
  loops' own time: 9.42 us -> 0 us
    reduce_scatter x2 -> x0, waiting for transfers between devices: 362 us -> none  [the longest x1 218 us: per_device(): lax.psum_scatter(qkv_grad_local, 'scan', scatter_dimension=2, tiled=True)]
    dot_general x62 -> x0, matrix products: 112 us -> none  [the longest x8 18.6 us: attend_back(): jnp.einsum('dq,dk->qk', chosen_grad, values, precision=PRECISE)]
    pallas_call x0 -> x2, Pallas kernels: none -> 103 us  [the longest x1 98 us: per_device(): pl.pallas_call(functools.partial(main_kernel, ns, nh), out_shape=(shape((...]
    gather x97 -> x0, local copies, waits for them, and re-layouts: 91.5 us -> none
    psum x1 -> x0, blocking collectives: 60.8 us -> none  [per_device(): gain_grad = lax.psum(jnp.sum(normed_grad * normed_local, axis=1), 'scan')]
    psum x1 -> x0, waiting for transfers between devices: 24.6 us -> none  [per_device(): lax.psum(partial_input.astype(jnp.bfloat16), 'head').astype(jnp.float32)]
    all_gather x2 -> x0, waiting for transfers between devices: 22.6 us -> none  [the longest x1 22.6 us: per_device(): full_rows = lax.all_gather(regrouped, 'head', axis=0, tiled=True)]
    all_to_all x4 -> x0, starting transfers between devices: 21.7 us -> none  [the longest x1 9.7 us: per_device(): lax.all_to_all(send_back, 'scan', split_axis=0, concat_axis=0, tiled=True)]
  transfers between devices with their start and end apart: 10 -> 0, of which waited for: 6 -> 0; matrix products, arithmetic and copies ran while one was open for 30% -> 0% of each run, Pallas kernels for 0% -> 0%
where the time goes in v2:
time: 104 us
  Pallas kernels  103 us (99%)
    pallas_call x1, Pallas kernels, per_device(): pl.pallas_call(functools.partial(main_kernel, ns, nh), out_shape=(shape((...  98 us
    pallas_call x1, Pallas kernels, per_device(): pl.pallas_call(functools.partial(slots_kernel, ns), out_shape=(shape((wid...  4.89 us

profile of v2, /device:TPU:1, one launch (start us, length us, event | category | flops | bytes accessed | tf_op | source)
XLA Modules:
  0.0 103.6 jit_solution(14362946890618820772)
XLA Ops:
  0.6 98.0 %patch_block.1 = (s32[32,128]{1,0:T(8,128)}, bf16[64,1024]{1,0:T(8,128)(2,1)}, bf16[32,64,128]{2,1,0:T(8,128)(2,1)}, f32[16,256]{1,0:T(8,128)}, f32[1,128]{1,0:T(1,128)}) custom-call(s32[1,1024]{1,0:T(1,128)} %bitcast.5, bf16[64,4224]{1,0:T(8,128)(2,1)} %points_ref.1, bf16[64,1024]{1,0:T(8,128)(2,1)} %cot_ref.1, f32[1,512]{1,0:T(1,128)} %bitcast.6, ...), custom_call_target="tpu_custom_call" | custom-call | tf_op jit(solution)/shard_map/patch_block/pallas_call | solution.py:454
  98.7 4.9 %slots.1 = (bf16[64,1024]{1,0:T(8,128)(2,1)}, bf16[64,4224]{1,0:T(8,128)(2,1)}, f32[3,16,64]{2,1,0:T(8,128)}, f32[16,64]{1,0:T(8,128)}, f32[1,64]{1,0:T(1,128)}) custom-call(s32[32,128]{1,0:T(8,128)} %get-tuple-element.15.sizes_ref, bf16[32,64,128]{2,1,0:T(8,128)(2,1)} %get-tuple-element.16.back_ref, bf16[64,1024]{1,0:T(8,128)(2,1)} %get-tuple-element.17.mixed_in, ...), custom_call_target="tpu_custom_call" | custom-call | tf_op jit(solution)/shard_map/slots/pallas_call | solution.py:511

commit v3 on v2

--- a/solution.py
+++ b/solution.py
@@ -10,12 +10,13 @@
 HD = 16
 BUCKET = 128
 EPS = 1e-05
-SPAN = 256
+SPAN = 1024
 LOG2E = 1.4426950408889634
 MESH = pl.DeviceIdType.MESH
 F32 = jnp.float32
 BF16 = jnp.bfloat16
 VMEM = pl.BlockSpec(memory_space=pltpu.VMEM)
+ANY = pl.BlockSpec(memory_space=pl.ANY)
 SMEM = pl.BlockSpec(memory_space=pltpu.SMEM)
 LIMIT = 56 * 1024 * 1024
 
@@ -72,23 +73,23 @@
 
 
 TALLY, POINTS, WGRAD, BACK, GAIN = range(5)
-COT, FULL, BRANCH, STATS, TWIN, PAIR = range(6)
+COT, FULL, BRANCH, STATS, TWIN, HALF, SUM = range(7)
 
 
 def main_kernel(
-    ns, nh, owner_ref, points_ref, cot_ref, gain_ref, weight_ref, outw_ref,
+    ns, nh, owner_ref, points_hbm, cot_hbm, gain_ref, weight_hbm, outw_hbm,
     sizes_ref, mixed_ref, back_ref, wsum_ref, gsum_ref,
     tall, tiles, offsets, windows, arrived, hots, full, cot, code_ref, gain_wide,
     normed, scaled, query, keys, value, gradc, context, grads, weights_all, shares,
-    key_t, value_t, branch_out, branch_in, part_out, twin_in, pair_out, pair_in, stats_out, stats_in,
-    wgrad_out, wgrad_in, gain_out, gain_in, buckets,
-    scan_send, scan_recv, head_send, head_recv,
+    key_t, value_t, branch_out, branch_in, part_out, twin_in, half_out, half_in, pair_out, pair_in, stats_out, stats_in,
+    wgrad_out, wgrad_in, gain_out, gain_in, buckets, points_ref, weight_ref, outw_ref,
+    local_sem, scan_send, scan_recv, head_send, head_recv,
 ):
     s, h = lax.axis_index("scan"), lax.axis_index("head")
     nx = nh // 2
     x, core = h // 2, lax.rem(h, 2)
     twin = x * 2 + 1 - core
-    width, rows = cot_ref.shape
+    width, rows = cot_hbm.shape
     channels = width * nh
     strip = channels // ns
     mine = aligned(h * width, width)
@@ -124,6 +125,13 @@
         block = ref.at[aligned(piece * width, width), :]
         return remote(block, block, head_send.at[which, slot], head_recv.at[which, piece], (s, to))
 
+    left, right, across = lax.rem(x + nx - 1, nx), lax.rem(x + 1, nx), lax.rem(x + 2, nx)
+    mid = width // 2
+
+    def half_piece(piece, half, slot, to):
+        block = full.at[aligned(piece * width + half * mid, mid), :]
+        return remote(block, block, head_send.at[HALF, slot], head_recv.at[HALF, slot], (s, to))
+
     def spread(which, ref):
         for j in (nx // 2, *[j for j in range(1, nx) if j != nx // 2]):
             push(which, ref, h, j, lax.rem(x + j, nx) * 2 + core).start()
@@ -160,15 +168,28 @@
 
     each(1, ns, greet_scan)
     each(1, nh, greet_head)
+    fetches = [
+        pltpu.make_async_copy(src, dst, local_sem.at[i])
+        for i, (src, dst) in enumerate(
+            [
+                (cot_hbm, cot.at[mine, :]),
+                (points_hbm, points_ref),
+                (outw_hbm, outw_ref),
+                (weight_hbm, weight_ref),
+            ]
+        )
+    ]
+    for fetch in fetches:
+        fetch.start()
     owners = owner_ref[...]
     hot = lax.broadcasted_iota(jnp.int32, (ns, rows), 0) == owners
     ones = jnp.where(hot, 1.0, 0.0)
     total = jnp.sum(jnp.where(hot, 1, 0), axis=1, keepdims=True)
     tall[...] = jnp.broadcast_to(total, (ns, 128))
-    cot[mine, :] = cot_ref[...]
     pl.semaphore_wait(barrier, ns + nh - 2)
 
     each(1, ns, lambda j: scan_copy(TALLY, j).start())
+    fetches[0].wait()
     spread(COT, cot)
     sizes_ref[pl.ds(s, 1), :] = tall[pl.ds(s, 1), :]
     before = jnp.where(
@@ -201,23 +222,38 @@
 
     def nth_group(i):
         half = (i + 1) // 2
-        shift = groups // 2 + jnp.where(lax.rem(i, 2) == 1, half, -half)
+        shift = groups // 2 + half * (lax.rem(i, 2) * 2 - 1)
         return lax.rem(s // 4 + shift + groups, groups)
 
-    def cut_and_send(i):
+    def send_group(which, group, last):
+        for t in range(4):
+            peer = group * 4 + t
+            if last:
+
+                @pl.when(peer != s)
+                def _():
+                    scan_copy(which, lax.rem(peer - s + ns, ns)).start()
+
+            else:
+                scan_copy(which, lax.rem(peer - s + ns, ns)).start()
+
+    def cut_and_send(i, last):
         group = nth_group(i)
-        places = [jnp.broadcast_to(tiles[pl.ds(group * 4 + t, 1), :], (16, 128)) for t in range(4)]
-        low = [jnp.zeros((width // 16, 16, 128), BF16) for t in range(4)]
-        high = [jnp.zeros((width // 16, 16, 128), BF16) for t in range(4)]
-        previous = [jnp.zeros((1, 16, 128), BF16) for t in range(4)]
+        places = [
+            jnp.broadcast_to(tiles[pl.ds(group * 4 + t, 1), :], (16, 128)).astype(F32).astype(BF16)
+            for t in range(4)
+        ]
+        zero = jnp.zeros((width // 16, 16, 128), BF16)
+
+        held = [zero] * 8
         for n in range(ns + 1):
-            tile = points_ref[:, 128 * n : 128 * (n + 1)].reshape(width // 16, 16, 128)
+            tile = points_ref[:, 128 * n : 128 * (n + 1)].reshape(zero.shape)
             for t in range(4):
-                here = jnp.where(places[t] == n, 1.0, 0.0).astype(BF16)[None]
-                high[t] = high[t] + tile * previous[t]
                 if n < ns:
-                    low[t] = low[t] + tile * here
-                previous[t] = here
+                    held[t] = jnp.where((places[t] == n)[None], tile, held[t])
+                if n > 0:
+                    held[4 + t] = jnp.where((places[t] == n - 1)[None], tile, held[4 + t])
+        low, high = held[:4], held[4:]
         for t in range(4):
             peer = group * 4 + t
             window = jnp.concatenate(
@@ -225,12 +261,12 @@
             )
             pick = jnp.where(span == offsets[pl.ds(peer, 1), :], 1.0, 0.0).astype(BF16)
             windows[peer] = dot_nn(window, pick).astype(BF16)
-
-            @pl.when(peer != s)
-            def _():
-                scan_copy(POINTS, lax.rem(peer - s + ns, ns)).start()
-
-    each(0, groups, cut_and_send)
+        send_group(POINTS, group, last)
+
+    for fetch in fetches[1:]:
+        fetch.wait()
+    each(0, groups - 1, lambda i: cut_and_send(i, False))
+    cut_and_send(groups - 1, True)
     arrived[pl.ds(s, 1)] = windows[pl.ds(s, 1)]
     code = code_ref[...]
 
@@ -251,16 +287,31 @@
         for t in range(4):
             source = group * 4 + t
 
-            @pl.when(source != s)
-            def _():
+            def landed(source=source):
                 scan_copy(POINTS, lax.rem(s - source + ns, ns)).wait_recv()
 
+            if i < groups - 1:
+                landed()
+            else:
+                pl.when(source != s)(landed)
         pieces = jnp.concatenate([arrived[group * 4 + t] for t in range(4)], axis=1)
         gathered = gathered + dot_nn(pieces, hots[aligned(group * 512, 512), :])
     full[mine, :] = gathered.astype(BF16)
-    spread(FULL, full)
-    relay(FULL, full)
-    arrive(FULL, full)
+    push(FULL, full, h, 1, right * 2 + core).start()
+    push(FULL, full, h, 3, left * 2 + core).start()
+    push(FULL, full, h, 0, twin).start()
+    for at, side, half, to in ((left, 1, 0, right), (right, 3, 1, left)):
+        piece = at * 2 + core
+        push(FULL, full, piece, nx + side, twin).wait_recv()
+        half_piece(piece, half, half, to * 2 + core).start()
+        push(FULL, full, piece, nx + side, twin).start()
+    for half in range(2):
+        half_piece(across * 2 + core, half, half, twin).wait_recv()
+        half_piece(across * 2 + core, half, 2 + half, twin).start()
+    for at in (x, left, right):
+        push(FULL, full, at * 2 + 1 - core, 0, twin).wait_recv()
+    for half in range(2):
+        half_piece(across * 2 + 1 - core, half, 2 + half, twin).wait_recv()
 
     floats = full[...].astype(F32)
     mean = jnp.sum(floats, axis=0, keepdims=True) * (1.0 / channels)
@@ -290,7 +341,8 @@
             ctx = (sums[:HD] + sums[HD : 2 * HD]) * share
             context[at, b : b + SPAN] = ctx
 
-    each(0, width // HD, forward)
+    for head in range(width // HD):
+        forward(head)
     context_b = context[...].astype(BF16)
     branch_out[...] = dot_tn(outw_ref[...], context_b).astype(BF16)
     each(1, nh, lambda j: head_copy(BRANCH, j).start())
@@ -326,7 +378,8 @@
         grads[k_at, :] = (key_grad[:HD] + key_grad[HD:]).astype(BF16)
         grads[v_at, :] = (value_grad[:HD] + value_grad[HD:]).astype(BF16)
 
-    each(0, width // HD, backward)
+    for head in range(width // HD):
+        backward(head)
 
     whole = jnp.concatenate([weight_ref[i] for i in range(3)], axis=0)
     part_out[...] = dot_tn(whole, grads[...]).astype(BF16)
@@ -336,14 +389,17 @@
         src = part_out.at[aligned((to * 2 + 1 - core) * width, width), :]
         return remote(src, twin_in.at[j], head_send.at[TWIN, j], head_recv.at[TWIN, j], (s, twin))
 
-    def pair_copy(j):
-        to = lax.rem(x + j, nx) * 2 + core
-        return remote(
-            pair_out.at[j], pair_in.at[j], head_send.at[PAIR, j], head_recv.at[PAIR, j], (s, to)
-        )
-
-    order = (*([nx // 2] if nx > 1 else []), *[j for j in range(1, nx) if j != nx // 2])
-    for j in (*order, 0):
+    def sum_copy(slot):
+        side, half = ((0, 0), (1, 1), (0, 1), (1, 0), (0, 0), (1, 1))[slot]
+        if slot < 2:
+            src, dst = half_out.at[side], half_in.at[side]
+        else:
+            rows_of = pl.ds(half * mid, mid)
+            src, dst = pair_out.at[side, rows_of, :], pair_in.at[side, rows_of, :]
+        to = (right, left)[side] * 2 + core
+        return remote(src, dst, head_send.at[SUM, slot], head_recv.at[SUM, slot], (s, to))
+
+    for j in (2, 1, 3, 0):
         twin_copy(j).start()
     weighted = part_out[...].astype(F32) * gain_wide[:, :1]
     stats_out[0:1, :] = jnp.sum(weighted, axis=0, keepdims=True)
@@ -355,9 +411,22 @@
         own = part_out[aligned((lax.rem(x + j, nx) * 2 + core) * width, width), :]
         return own.astype(F32) + twin_in[j].astype(F32)
 
-    for j in order:
-        pair_out[j] = pair_sum(j).astype(BF16)
-        pair_copy(j).start()
+    far_sum = pair_sum(2).astype(BF16)
+    half_out[0] = far_sum[:mid]
+    half_out[1] = far_sum[mid:]
+    sum_copy(0).start()
+    sum_copy(1).start()
+    to_right, to_left = pair_sum(1), pair_sum(3)
+    pair_out[0, mid:, :] = to_right[mid:].astype(BF16)
+    sum_copy(2).start()
+    pair_out[1, :mid, :] = to_left[:mid].astype(BF16)
+    sum_copy(3).start()
+    sum_copy(0).wait_recv()
+    pair_out[0, :mid, :] = (to_right[:mid] + half_in[0].astype(F32)).astype(BF16)
+    sum_copy(4).start()
+    sum_copy(1).wait_recv()
+    pair_out[1, mid:, :] = (to_left[mid:] + half_in[1].astype(F32)).astype(BF16)
+    sum_copy(5).start()
     normed_grad = pair_sum(0)
     wgrad_out[:, : 3 * width] = dot_nt(scaled[...], grads[...]).astype(BF16)
     wgrad_out[:, 3 * width :] = dot_nt(cot[...], context_b).astype(BF16)
@@ -372,24 +441,20 @@
     stats = stats_out[...]
     for i in range(1, nh):
         stats = stats + stats_in[lax.rem(h + i, nh)]
-    for j in order:
-        pair_copy(j).wait_recv()
-        normed_grad = normed_grad + pair_in[j].astype(F32)
+    for slot in range(2, 6):
+        sum_copy(slot).wait_recv()
+    normed_grad = normed_grad + pair_in[0].astype(F32) + pair_in[1].astype(F32)
     normed_own = normed[mine, :]
     first, second = stats[0:1] * (1.0 / channels), stats[1:2] * (1.0 / channels)
     grad = inv * (normed_grad * gain_wide[mine, :1] - first - normed_own * second)
-    points_grad = (cot_ref[...].astype(F32) + grad).astype(BF16)
+    points_grad = (cot[mine, :].astype(F32) + grad).astype(BF16)
 
     for i in range(groups):
         group = nth_group(i)
         block = dot_nt(points_grad, hots[aligned(group * 512, 512), :]).astype(BF16)
         for t in range(4):
-            peer = group * 4 + t
-            buckets[peer] = block[:, 128 * t : 128 * (t + 1)]
-
-            @pl.when(peer != s)
-            def _():
-                scan_copy(BACK, lax.rem(peer - s + ns, ns)).start()
+            buckets[group * 4 + t] = block[:, 128 * t : 128 * (t + 1)]
+        send_group(BACK, group, i == groups - 1)
 
     back_ref[pl.ds(s, 1)] = buckets[pl.ds(s, 1)]
     product = normed_grad * normed_own
@@ -405,11 +470,14 @@
     each(1, ns, lambda j: scan_copy(GAIN, j).wait())
     gsum_ref[...] = jnp.sum(gain_in[...], axis=0)
     sent(COT, cot)
-    sent(FULL, full)
-    for j in (*order, 0):
+    for slot in (0, 1, 3, nx + 1, nx + 3):
+        push(FULL, full, h, slot, twin).wait_send()
+    for slot in range(4):
+        half_piece(h, 0, slot, twin).wait_send()
+    for j in range(nx):
         twin_copy(j).wait_send()
-    for j in order:
-        pair_copy(j).wait_send()
+    for slot in range(6):
+        sum_copy(slot).wait_send()
     each(1, ns, lambda j: scan_copy(POINTS, j).wait_send())
     each(1, ns, lambda j: scan_copy(BACK, j).wait())
 
@@ -460,7 +528,7 @@
             shape((strip, 4 * width), F32),
             shape((1, 128), F32),
         ),
-        in_specs=[VMEM] * 6,
+        in_specs=[VMEM, ANY, ANY, VMEM, ANY, ANY],
         out_specs=(VMEM,) * 5,
         scratch_shapes=[
             vmem((ns, 128), jnp.int32),
@@ -489,8 +557,10 @@
             vmem((nh, width, rows), BF16),
             vmem((channels, rows), BF16),
             vmem((nx, width, rows), BF16),
-            vmem((nx, width, rows), BF16),
-            vmem((nx, width, rows), BF16),
+            vmem((2, width // 2, rows), BF16),
+            vmem((2, width // 2, rows), BF16),
+            vmem((2, width, rows), BF16),
+            vmem((2, width, rows), BF16),
             vmem((2, rows), F32),
             vmem((nh, 2, rows), F32),
             vmem((channels, 4 * width), BF16),
@@ -498,10 +568,14 @@
             vmem((1, 128), F32),
             vmem((ns, 1, 128), F32),
             vmem((ns, width, BUCKET), BF16),
+            vmem((width, slot_count), BF16),
+            vmem((3, width, channels), BF16),
+            vmem((width, channels), BF16),
+            dma((4,)),
             dma((5, ns)),
             dma((5, ns)),
-            dma((6, nh)),
-            dma((6, nh)),
+            dma((7, nh)),
+            dma((7, nh)),
         ],
         compiler_params=pltpu.CompilerParams(
             collective_id=1, has_side_effects=True, vmem_limit_bytes=LIMIT

time: 104 us -> 101 us (0.971)
  Pallas kernels: 103 us -> 100 us
    pallas_call x1, Pallas kernels: 98 us -> 95.5 us  [per_device(): pl.pallas_call(functools.partial(main_kernel, ns, nh), out_shape=(shape((...]
where the time goes in v3:
time: 101 us
  Pallas kernels  100 us (99%)
    pallas_call x1, Pallas kernels, per_device(): pl.pallas_call(functools.partial(main_kernel, ns, nh), out_shape=(shape((...  95.5 us
    pallas_call x1, Pallas kernels, per_device(): pl.pallas_call(functools.partial(slots_kernel, ns), out_shape=(shape((wid...  4.89 us

profile of v3, /device:TPU:1, one launch (start us, length us, event | category | flops | bytes accessed | tf_op | source)
XLA Modules:
  0.0 101.0 jit_solution(7206484337699647856)
XLA Ops:
  0.6 95.5 %patch_block.1 = (s32[32,128]{1,0:T(8,128)}, bf16[64,1024]{1,0:T(8,128)(2,1)}, bf16[32,64,128]{2,1,0:T(8,128)(2,1)}, f32[16,256]{1,0:T(8,128)}, f32[1,128]{1,0:T(1,128)}) custom-call(s32[1,1024]{1,0:T(1,128)} %bitcast.5, bf16[64,4224]{1,0:T(8,128)(2,1)} %points_hbm.1, bf16[64,1024]{1,0:T(8,128)(2,1)} %cot_hbm.1, f32[1,512]{1,0:T(1,128)} %bitcast.6, ...), custom_call_target="tpu_custom_call" | custom-call | tf_op jit(solution)/shard_map/patch_block/pallas_call | solution.py:522
  96.1 4.9 %slots.1 = (bf16[64,1024]{1,0:T(8,128)(2,1)}, bf16[64,4224]{1,0:T(8,128)(2,1)}, f32[3,16,64]{2,1,0:T(8,128)}, f32[16,64]{1,0:T(8,128)}, f32[1,64]{1,0:T(1,128)}) custom-call(s32[32,128]{1,0:T(8,128)} %get-tuple-element.15.sizes_ref, bf16[32,64,128]{2,1,0:T(8,128)(2,1)} %get-tuple-element.16.back_ref, bf16[64,1024]{1,0:T(8,128)(2,1)} %get-tuple-element.17.mixed_in, ...), custom_call_target="tpu_custom_call" | custom-call | tf_op jit(solution)/shard_map/slots/pallas_call | solution.py:585

commit v4 on v3

--- a/solution.py
+++ b/solution.py
@@ -64,16 +64,16 @@
     return pl.ds(pl.multiple_of(first, size), size)
 
 
-def each(first, last, act):
+def each(first, last, act, unroll=True):
     def body(j, carry):
         act(j)
         return carry
 
-    lax.fori_loop(first, last, body, 0)
+    lax.fori_loop(first, last, body, 0, unroll=unroll)
 
 
 TALLY, POINTS, WGRAD, BACK, GAIN = range(5)
-COT, FULL, BRANCH, STATS, TWIN, HALF, SUM = range(7)
+COT, FULL, STATS, HALF, TWIN, _, SUM, _ = range(8)
 
 
 def main_kernel(
@@ -81,7 +81,7 @@
     sizes_ref, mixed_ref, back_ref, wsum_ref, gsum_ref,
     tall, tiles, offsets, windows, arrived, hots, full, cot, code_ref, gain_wide,
     normed, scaled, query, keys, value, gradc, context, grads, weights_all, shares,
-    key_t, value_t, branch_out, branch_in, part_out, twin_in, half_out, half_in, pair_out, pair_in, stats_out, stats_in,
+    key_t, value_t, branch_out, near, part_out, twin_in, half_out, half_in, pair_out, pair_in, stats_out, stats_in,
     wgrad_out, wgrad_in, gain_out, gain_in, buckets, points_ref, weight_ref, outw_ref,
     local_sem, scan_send, scan_recv, head_send, head_recv,
 ):
@@ -113,13 +113,11 @@
             src, dst = gain_out, gain_in.at[s]
         return remote(src, dst, scan_send.at[which, j], scan_recv.at[which, j], (peer, h))
 
-    def head_copy(which, j):
+    def stats_copy(j):
         peer = lax.rem(h + j, nh)
-        if which == BRANCH:
-            src, dst = branch_out.at[aligned(peer * width, width), :], branch_in.at[h]
-        else:
-            src, dst = stats_out, stats_in.at[h]
-        return remote(src, dst, head_send.at[which, j], head_recv.at[which, j], (s, peer))
+        return remote(
+            stats_out, stats_in.at[h], head_send.at[STATS, j], head_recv.at[STATS, j], (s, peer)
+        )
 
     def push(which, ref, piece, slot, to):
         block = ref.at[aligned(piece * width, width), :]
@@ -153,6 +151,66 @@
             push(which, ref, h, j, twin).wait_send()
             push(which, ref, h, nx + j, twin).wait_send()
         push(which, ref, h, 0, twin).wait_send()
+
+    def twin_copy(k, j):
+        to = lax.rem(x + j, nx)
+        src = (part_out, branch_out)[k].at[aligned((to * 2 + 1 - core) * width, width), :]
+        dst = twin_in.at[k, j]
+        return remote(src, dst, head_send.at[TWIN + k, j], head_recv.at[TWIN + k, j], (s, twin))
+
+    def sum_copy(k, slot):
+        side, half = ((0, 0), (1, 1), (0, 1), (1, 0), (0, 0), (1, 1))[slot]
+        if slot < 2:
+            src, dst = half_out.at[k, side], half_in.at[k, side]
+        else:
+            rows_of = pl.ds(half * mid, mid)
+            src, dst = pair_out.at[k, side, rows_of, :], pair_in.at[k, side, rows_of, :]
+        to = (right, left)[side] * 2 + core
+        return remote(src, dst, head_send.at[SUM + k, slot], head_recv.at[SUM + k, slot], (s, to))
+
+    def pair_sum(k, j):
+        twin_copy(k, j).wait_recv()
+        ref = (part_out, branch_out)[k]
+        own = ref[aligned((lax.rem(x + j, nx) * 2 + core) * width, width), :]
+        return own.astype(F32) + twin_in[k, j].astype(F32)
+
+    def sum_begin(k):
+        for j in (2, 1, 3, 0):
+            twin_copy(k, j).start()
+
+    def sum_far(k):
+        far_sum = pair_sum(k, 2).astype(BF16)
+        half_out[k, 0] = far_sum[:mid]
+        half_out[k, 1] = far_sum[mid:]
+        sum_copy(k, 0).start()
+        sum_copy(k, 1).start()
+        to_right, to_left = pair_sum(k, 1), pair_sum(k, 3)
+        pair_out[k, 0, mid:, :] = to_right[mid:].astype(BF16)
+        sum_copy(k, 2).start()
+        pair_out[k, 1, :mid, :] = to_left[:mid].astype(BF16)
+        sum_copy(k, 3).start()
+        near[k, 0] = to_right[:mid]
+        near[k, 1] = to_left[mid:]
+
+    def sum_near(k):
+        sum_copy(k, 0).wait_recv()
+        pair_out[k, 0, :mid, :] = (near[k, 0] + half_in[k, 0].astype(F32)).astype(BF16)
+        sum_copy(k, 4).start()
+        sum_copy(k, 1).wait_recv()
+        pair_out[k, 1, mid:, :] = (near[k, 1] + half_in[k, 1].astype(F32)).astype(BF16)
+        sum_copy(k, 5).start()
+
+    def sum_end(k):
+        own = pair_sum(k, 0)
+        for slot in range(2, 6):
+            sum_copy(k, slot).wait_recv()
+        return own + pair_in[k, 0].astype(F32) + pair_in[k, 1].astype(F32)
+
+    def sum_sent(k):
+        for j in range(nx):
+            twin_copy(k, j).wait_send()
+        for slot in range(6):
+            sum_copy(k, slot).wait_send()
 
     barrier = pltpu.get_barrier_semaphore()
 
@@ -265,7 +323,7 @@
 
     for fetch in fetches[1:]:
         fetch.wait()
-    each(0, groups - 1, lambda i: cut_and_send(i, False))
+    each(0, groups - 1, lambda i: cut_and_send(i, False), False)
     cut_and_send(groups - 1, True)
     arrived[pl.ds(s, 1)] = windows[pl.ds(s, 1)]
     code = code_ref[...]
@@ -345,7 +403,7 @@
         forward(head)
     context_b = context[...].astype(BF16)
     branch_out[...] = dot_tn(outw_ref[...], context_b).astype(BF16)
-    each(1, nh, lambda j: head_copy(BRANCH, j).start())
+    sum_begin(1)
 
     def backward(head):
         at = aligned(head * HD, HD)
@@ -380,70 +438,33 @@
 
     for head in range(width // HD):
         backward(head)
+        if head == 0:
+            sum_far(1)
+        elif head == 1:
+            sum_near(1)
 
     whole = jnp.concatenate([weight_ref[i] for i in range(3)], axis=0)
     part_out[...] = dot_tn(whole, grads[...]).astype(BF16)
 
-    def twin_copy(j):
-        to = lax.rem(x + j, nx)
-        src = part_out.at[aligned((to * 2 + 1 - core) * width, width), :]
-        return remote(src, twin_in.at[j], head_send.at[TWIN, j], head_recv.at[TWIN, j], (s, twin))
-
-    def sum_copy(slot):
-        side, half = ((0, 0), (1, 1), (0, 1), (1, 0), (0, 0), (1, 1))[slot]
-        if slot < 2:
-            src, dst = half_out.at[side], half_in.at[side]
-        else:
-            rows_of = pl.ds(half * mid, mid)
-            src, dst = pair_out.at[side, rows_of, :], pair_in.at[side, rows_of, :]
-        to = (right, left)[side] * 2 + core
-        return remote(src, dst, head_send.at[SUM, slot], head_recv.at[SUM, slot], (s, to))
-
-    for j in (2, 1, 3, 0):
-        twin_copy(j).start()
+    sum_begin(0)
     weighted = part_out[...].astype(F32) * gain_wide[:, :1]
     stats_out[0:1, :] = jnp.sum(weighted, axis=0, keepdims=True)
     stats_out[1:2, :] = jnp.sum(weighted * normed[...], axis=0, keepdims=True)
-    each(1, nh, lambda j: head_copy(STATS, j).start())
-
-    def pair_sum(j):
-        twin_copy(j).wait_recv()
-        own = part_out[aligned((lax.rem(x + j, nx) * 2 + core) * width, width), :]
-        return own.astype(F32) + twin_in[j].astype(F32)
-
-    far_sum = pair_sum(2).astype(BF16)
-    half_out[0] = far_sum[:mid]
-    half_out[1] = far_sum[mid:]
-    sum_copy(0).start()
-    sum_copy(1).start()
-    to_right, to_left = pair_sum(1), pair_sum(3)
-    pair_out[0, mid:, :] = to_right[mid:].astype(BF16)
-    sum_copy(2).start()
-    pair_out[1, :mid, :] = to_left[:mid].astype(BF16)
-    sum_copy(3).start()
-    sum_copy(0).wait_recv()
-    pair_out[0, :mid, :] = (to_right[:mid] + half_in[0].astype(F32)).astype(BF16)
-    sum_copy(4).start()
-    sum_copy(1).wait_recv()
-    pair_out[1, mid:, :] = (to_left[mid:] + half_in[1].astype(F32)).astype(BF16)
-    sum_copy(5).start()
-    normed_grad = pair_sum(0)
+    each(1, nh, lambda j: stats_copy(j).start())
+
+    sum_far(0)
+    sum_near(0)
     wgrad_out[:, : 3 * width] = dot_nt(scaled[...], grads[...]).astype(BF16)
     wgrad_out[:, 3 * width :] = dot_nt(cot[...], context_b).astype(BF16)
     each(1, ns, lambda j: scan_copy(WGRAD, j).start())
     wgrad_in[pl.ds(s, 1)] = wgrad_out[aligned(s * strip, strip), :][None]
-    each(1, nh, lambda j: head_copy(BRANCH, j).wait())
-    branch = branch_out[mine, :].astype(F32)
-    for i in range(1, nh):
-        branch = branch + branch_in[lax.rem(h + i, nh)].astype(F32)
+    branch = sum_end(1)
     mixed_ref[...] = (full[mine, :].astype(F32) + branch).astype(BF16)
-    each(1, nh, lambda j: head_copy(STATS, j).wait())
+    each(1, nh, lambda j: stats_copy(j).wait())
     stats = stats_out[...]
     for i in range(1, nh):
         stats = stats + stats_in[lax.rem(h + i, nh)]
-    for slot in range(2, 6):
-        sum_copy(slot).wait_recv()
-    normed_grad = normed_grad + pair_in[0].astype(F32) + pair_in[1].astype(F32)
+    normed_grad = sum_end(0)
     normed_own = normed[mine, :]
     first, second = stats[0:1] * (1.0 / channels), stats[1:2] * (1.0 / channels)
     grad = inv * (normed_grad * gain_wide[mine, :1] - first - normed_own * second)
@@ -474,10 +495,8 @@
         push(FULL, full, h, slot, twin).wait_send()
     for slot in range(4):
         half_piece(h, 0, slot, twin).wait_send()
-    for j in range(nx):
-        twin_copy(j).wait_send()
-    for slot in range(6):
-        sum_copy(slot).wait_send()
+    sum_sent(0)
+    sum_sent(1)
     each(1, ns, lambda j: scan_copy(POINTS, j).wait_send())
     each(1, ns, lambda j: scan_copy(BACK, j).wait())
 
@@ -554,13 +573,13 @@
             vmem((rows, 6 * HD), BF16),
             vmem((rows, 7 * HD), BF16),
             vmem((channels, rows), BF16),
-            vmem((nh, width, rows), BF16),
+            vmem((2, 2, width // 2, rows), F32),
             vmem((channels, rows), BF16),
-            vmem((nx, width, rows), BF16),
-            vmem((2, width // 2, rows), BF16),
-            vmem((2, width // 2, rows), BF16),
-            vmem((2, width, rows), BF16),
-            vmem((2, width, rows), BF16),
+            vmem((2, nx, width, rows), BF16),
+            vmem((2, 2, width // 2, rows), BF16),
+            vmem((2, 2, width // 2, rows), BF16),
+            vmem((2, 2, width, rows), BF16),
+            vmem((2, 2, width, rows), BF16),
             vmem((2, rows), F32),
             vmem((nh, 2, rows), F32),
             vmem((channels, 4 * width), BF16),
@@ -574,8 +593,8 @@
             dma((4,)),
             dma((5, ns)),
             dma((5, ns)),
-            dma((7, nh)),
-            dma((7, nh)),
+            dma((8, nh)),
+            dma((8, nh)),
         ],
         compiler_params=pltpu.CompilerParams(
             collective_id=1, has_side_effects=True, vmem_limit_bytes=LIMIT

time: 101 us -> 97.4 us (0.964)
  Pallas kernels: 100 us -> 96.6 us
    pallas_call x1, Pallas kernels: 95.5 us -> 91.7 us  [per_device(): pl.pallas_call(functools.partial(main_kernel, ns, nh), out_shape=(shape((...]
where the time goes in v4:
time: 97.4 us; the launch traced here: 97.3 us
  Pallas kernels  96.6 us (99%)
    pallas_call x1, Pallas kernels, per_device(): pl.pallas_call(functools.partial(main_kernel, ns, nh), out_shape=(shape((...  91.7 us
    pallas_call x1, Pallas kernels, per_device(): pl.pallas_call(functools.partial(slots_kernel, ns), out_shape=(shape((wid...  4.89 us

profile of v4, /device:TPU:1, one launch (start us, length us, event | category | flops | bytes accessed | tf_op | source)
XLA Modules:
  0.0 97.3 jit_solution(9571603766986860084)
XLA Ops:
  0.6 91.7 %patch_block.1 = (s32[32,128]{1,0:T(8,128)}, bf16[64,1024]{1,0:T(8,128)(2,1)}, bf16[32,64,128]{2,1,0:T(8,128)(2,1)}, f32[16,256]{1,0:T(8,128)}, f32[1,128]{1,0:T(1,128)}) custom-call(s32[1,1024]{1,0:T(1,128)} %bitcast.5, bf16[64,4224]{1,0:T(8,128)(2,1)} %points_hbm.1, bf16[64,1024]{1,0:T(8,128)(2,1)} %cot_hbm.1, f32[1,512]{1,0:T(1,128)} %bitcast.6, ...), custom_call_target="tpu_custom_call" | custom-call | tf_op jit(solution)/shard_map/patch_block/pallas_call | solution.py:541
  92.4 4.9 %slots.1 = (bf16[64,1024]{1,0:T(8,128)(2,1)}, bf16[64,4224]{1,0:T(8,128)(2,1)}, f32[3,16,64]{2,1,0:T(8,128)}, f32[16,64]{1,0:T(8,128)}, f32[1,64]{1,0:T(1,128)}) custom-call(s32[32,128]{1,0:T(8,128)} %get-tuple-element.15.sizes_ref, bf16[32,64,128]{2,1,0:T(8,128)(2,1)} %get-tuple-element.16.back_ref, bf16[64,1024]{1,0:T(8,128)(2,1)} %get-tuple-element.17.mixed_in, ...), custom_call_target="tpu_custom_call" | custom-call | tf_op jit(solution)/shard_map/slots/pallas_call | solution.py:604

commit v5 on v4

--- a/solution.py
+++ b/solution.py
@@ -263,6 +263,15 @@
         rank = jnp.sum(running * part, axis=0, keepdims=True)
         code_ref[:, b : b + 128] = owners[:, b : b + 128] * BUCKET + rank.astype(jnp.int32)
         carried = carried + jnp.sum(part, axis=1, keepdims=True)
+    code = code_ref[...]
+
+    def build(i):
+        first = pl.multiple_of(i * 256, 256)
+        hots[pl.ds(first, 256), :] = hot_block(code, first, 256)
+
+    each(0, ns // 2, build, False)
+    gain = jnp.transpose(jnp.broadcast_to(gain_ref[...], (8, channels)))[:, :1]
+    gain_wide[...] = jnp.broadcast_to(gain, gain_wide.shape)
     each(1, ns, lambda j: scan_copy(TALLY, j).wait())
 
     earlier = jnp.where(
@@ -326,18 +335,7 @@
     each(0, groups - 1, lambda i: cut_and_send(i, False), False)
     cut_and_send(groups - 1, True)
     arrived[pl.ds(s, 1)] = windows[pl.ds(s, 1)]
-    code = code_ref[...]
-
-    def build(i):
-        first = pl.multiple_of(i * 256, 256)
-        hots[pl.ds(first, 256), :] = hot_block(code, first, 256)
-
-    each(0, ns // 2, build)
     relay(COT, cot)
-    gain = jnp.transpose(jnp.broadcast_to(gain_ref[...], (8, channels)))[:, :1]
-    gain_wide[...] = jnp.broadcast_to(gain, gain_wide.shape)
-    arrive(COT, cot)
-    gradc[...] = dot_nn(outw_ref[...], cot[...])
 
     gathered = jnp.zeros((width, rows), F32)
     for i in range(groups):
@@ -358,6 +356,8 @@
     push(FULL, full, h, 1, right * 2 + core).start()
     push(FULL, full, h, 3, left * 2 + core).start()
     push(FULL, full, h, 0, twin).start()
+    arrive(COT, cot)
+    gradc[...] = dot_nn(outw_ref[...], cot[...])
     for at, side, half, to in ((left, 1, 0, right), (right, 3, 1, left)):
         piece = at * 2 + core
         push(FULL, full, piece, nx + side, twin).wait_recv()
@@ -447,16 +447,16 @@
     part_out[...] = dot_tn(whole, grads[...]).astype(BF16)
 
     sum_begin(0)
+    wgrad_out[:, : 3 * width] = dot_nt(scaled[...], grads[...]).astype(BF16)
+    wgrad_out[:, 3 * width :] = dot_nt(cot[...], context_b).astype(BF16)
+    each(1, ns, lambda j: scan_copy(WGRAD, j).start())
+    sum_far(0)
     weighted = part_out[...].astype(F32) * gain_wide[:, :1]
     stats_out[0:1, :] = jnp.sum(weighted, axis=0, keepdims=True)
     stats_out[1:2, :] = jnp.sum(weighted * normed[...], axis=0, keepdims=True)
     each(1, nh, lambda j: stats_copy(j).start())
 
-    sum_far(0)
     sum_near(0)
-    wgrad_out[:, : 3 * width] = dot_nt(scaled[...], grads[...]).astype(BF16)
-    wgrad_out[:, 3 * width :] = dot_nt(cot[...], context_b).astype(BF16)
-    each(1, ns, lambda j: scan_copy(WGRAD, j).start())
     wgrad_in[pl.ds(s, 1)] = wgrad_out[aligned(s * strip, strip), :][None]
     branch = sum_end(1)
     mixed_ref[...] = (full[mine, :].astype(F32) + branch).astype(BF16)
@@ -519,7 +519,7 @@
         slots[:, at] = slots[:, at] + pltpu.roll(wide, off, 1)
         return begin + size
 
-    lax.fori_loop(0, ns, one, jnp.int32(0))
+    lax.fori_loop(0, ns, one, jnp.int32(0), unroll=8)
     owned_ref[...] = slots[...].astype(BF16)
     mixed_ref[...] = mixed_in[...]
     for i in range(3):

time: 97.4 us -> 94.4 us (0.969)
  Pallas kernels: 96.6 us -> 93.6 us
    pallas_call x1, Pallas kernels: 4.89 us -> 2.71 us  [per_device(): pl.pallas_call(functools.partial(slots_kernel, ns), out_shape=(shape((wid...]
where the time goes in v5:
time: 94.4 us; the launch traced here: 94.3 us
  Pallas kernels  93.6 us (99%)
    pallas_call x1, Pallas kernels, per_device(): pl.pallas_call(functools.partial(main_kernel, ns, nh), out_shape=(shape((...  90.9 us
    pallas_call x1, Pallas kernels, per_device(): pl.pallas_call(functools.partial(slots_kernel, ns), out_shape=(shape((wid...  2.71 us

profile of v5, /device:TPU:1, one launch (start us, length us, event | category | flops | bytes accessed | tf_op | source)
XLA Modules:
  0.0 94.3 jit_solution(7348504562559672455)
XLA Ops:
  0.6 90.9 %patch_block.1 = (s32[32,128]{1,0:T(8,128)}, bf16[64,1024]{1,0:T(8,128)(2,1)}, bf16[32,64,128]{2,1,0:T(8,128)(2,1)}, f32[16,256]{1,0:T(8,128)}, f32[1,128]{1,0:T(1,128)}) custom-call(s32[1,1024]{1,0:T(1,128)} %bitcast.5, bf16[64,4224]{1,0:T(8,128)(2,1)} %points_hbm.1, bf16[64,1024]{1,0:T(8,128)(2,1)} %cot_hbm.1, f32[1,512]{1,0:T(1,128)} %bitcast.6, ...), custom_call_target="tpu_custom_call" | custom-call | tf_op jit(solution)/shard_map/patch_block/pallas_call | solution.py:541
  91.5 2.7 %slots.1 = (bf16[64,1024]{1,0:T(8,128)(2,1)}, bf16[64,4224]{1,0:T(8,128)(2,1)}, f32[3,16,64]{2,1,0:T(8,128)}, f32[16,64]{1,0:T(8,128)}, f32[1,64]{1,0:T(1,128)}) custom-call(s32[32,128]{1,0:T(8,128)} %get-tuple-element.15.sizes_ref, bf16[32,64,128]{2,1,0:T(8,128)(2,1)} %get-tuple-element.16.back_ref, bf16[64,1024]{1,0:T(8,128)(2,1)} %get-tuple-element.17.mixed_in, ...), custom_call_target="tpu_custom_call" | custom-call | tf_op jit(solution)/shard_map/slots/pallas_call | solution.py:604

commit v6 on v5

--- a/solution.py
+++ b/solution.py
@@ -304,19 +304,19 @@
             else:
                 scan_copy(which, lax.rem(peer - s + ns, ns)).start()
 
-    def cut_and_send(i, last):
-        group = nth_group(i)
+    def cut(group):
+        high_of = group * 4 + 4
         places = [
-            jnp.broadcast_to(tiles[pl.ds(group * 4 + t, 1), :], (16, 128)).astype(F32).astype(BF16)
+            jnp.broadcast_to(tiles[group * 4 + t : group * 4 + t + 1, :], (16, 128)).astype(F32).astype(BF16)
             for t in range(4)
         ]
         zero = jnp.zeros((width // 16, 16, 128), BF16)
 
         held = [zero] * 8
-        for n in range(ns + 1):
+        for n in range(high_of + 1):
             tile = points_ref[:, 128 * n : 128 * (n + 1)].reshape(zero.shape)
             for t in range(4):
-                if n < ns:
+                if n < high_of:
                     held[t] = jnp.where((places[t] == n)[None], tile, held[t])
                 if n > 0:
                     held[4 + t] = jnp.where((places[t] == n - 1)[None], tile, held[4 + t])
@@ -326,8 +326,12 @@
             window = jnp.concatenate(
                 [low[t].reshape(width, 128), high[t].reshape(width, 128)], axis=1
             )
-            pick = jnp.where(span == offsets[pl.ds(peer, 1), :], 1.0, 0.0).astype(BF16)
+            pick = jnp.where(span == offsets[peer : peer + 1, :], 1.0, 0.0).astype(BF16)
             windows[peer] = dot_nn(window, pick).astype(BF16)
+
+    def cut_and_send(i, last):
+        group = nth_group(i)
+        lax.switch(group, [functools.partial(cut, n) for n in range(groups)])
         send_group(POINTS, group, last)
 
     for fetch in fetches[1:]:

time: 94.4 us -> 94.3 us (level)
  no operation moved by 1% of the time
where the time goes in v6:
time: 94.3 us; the launch traced here: 94.2 us
  Pallas kernels  93.5 us (99%)
    pallas_call x1, Pallas kernels, per_device(): pl.pallas_call(functools.partial(main_kernel, ns, nh), out_shape=(shape((...  90.8 us
    pallas_call x1, Pallas kernels, per_device(): pl.pallas_call(functools.partial(slots_kernel, ns), out_shape=(shape((wid...  2.71 us

profile of v6, /device:TPU:1, one launch (start us, length us, event | category | flops | bytes accessed | tf_op | source)
XLA Modules:
  0.0 94.2 jit_solution(527343606657699344)
XLA Ops:
  0.6 90.8 %patch_block.1 = (s32[32,128]{1,0:T(8,128)}, bf16[64,1024]{1,0:T(8,128)(2,1)}, bf16[32,64,128]{2,1,0:T(8,128)(2,1)}, f32[16,256]{1,0:T(8,128)}, f32[1,128]{1,0:T(1,128)}) custom-call(s32[1,1024]{1,0:T(1,128)} %bitcast.5, bf16[64,4224]{1,0:T(8,128)(2,1)} %points_hbm.1, bf16[64,1024]{1,0:T(8,128)(2,1)} %cot_hbm.1, f32[1,512]{1,0:T(1,128)} %bitcast.6, ...), custom_call_target="tpu_custom_call" | custom-call | tf_op jit(solution)/shard_map/patch_block/pallas_call | solution.py:545
  91.5 2.7 %slots.1 = (bf16[64,1024]{1,0:T(8,128)(2,1)}, bf16[64,4224]{1,0:T(8,128)(2,1)}, f32[3,16,64]{2,1,0:T(8,128)}, f32[16,64]{1,0:T(8,128)}, f32[1,64]{1,0:T(1,128)}) custom-call(s32[32,128]{1,0:T(8,128)} %get-tuple-element.15.sizes_ref, bf16[32,64,128]{2,1,0:T(8,128)(2,1)} %get-tuple-element.16.back_ref, bf16[64,1024]{1,0:T(8,128)(2,1)} %get-tuple-element.17.mixed_in, ...), custom_call_target="tpu_custom_call" | custom-call | tf_op jit(solution)/shard_map/slots/pallas_call | solution.py:608

commit v7 on v5

--- a/solution.py
+++ b/solution.py
@@ -353,16 +353,22 @@
         pieces = jnp.concatenate([arrived[group * 4 + t] for t in range(4)], axis=1)
         gathered = gathered + dot_nn(pieces, hots[aligned(group * 512, 512), :])
     full[mine, :] = gathered.astype(BF16)
-    push(FULL, full, h, 1, right * 2 + core).start()
-    push(FULL, full, h, 3, left * 2 + core).start()
+    half_piece(h, 0, 4, right * 2 + core).start()
+    half_piece(h, 1, 6, left * 2 + core).start()
+    half_piece(h, 1, 5, right * 2 + core).start()
+    half_piece(h, 0, 7, left * 2 + core).start()
     push(FULL, full, h, 0, twin).start()
+    from_left, from_right = left * 2 + core, right * 2 + core
+    half_piece(from_left, 0, 4, twin).wait_recv()
+    half_piece(from_left, 0, 0, right * 2 + core).start()
+    half_piece(from_right, 1, 6, twin).wait_recv()
+    half_piece(from_right, 1, 1, left * 2 + core).start()
+    half_piece(from_left, 1, 5, twin).wait_recv()
+    push(FULL, full, from_left, nx + 1, twin).start()
+    half_piece(from_right, 0, 7, twin).wait_recv()
+    push(FULL, full, from_right, nx + 3, twin).start()
     arrive(COT, cot)
     gradc[...] = dot_nn(outw_ref[...], cot[...])
-    for at, side, half, to in ((left, 1, 0, right), (right, 3, 1, left)):
-        piece = at * 2 + core
-        push(FULL, full, piece, nx + side, twin).wait_recv()
-        half_piece(piece, half, half, to * 2 + core).start()
-        push(FULL, full, piece, nx + side, twin).start()
     for half in range(2):
         half_piece(across * 2 + core, half, half, twin).wait_recv()
         half_piece(across * 2 + core, half, 2 + half, twin).start()
@@ -491,9 +497,9 @@
     each(1, ns, lambda j: scan_copy(GAIN, j).wait())
     gsum_ref[...] = jnp.sum(gain_in[...], axis=0)
     sent(COT, cot)
-    for slot in (0, 1, 3, nx + 1, nx + 3):
+    for slot in (0, nx + 1, nx + 3):
         push(FULL, full, h, slot, twin).wait_send()
-    for slot in range(4):
+    for slot in range(8):
         half_piece(h, 0, slot, twin).wait_send()
     sum_sent(0)
     sum_sent(1)

time: 94.4 us -> 93.7 us (level)
  no operation moved by 1% of the time
where the time goes in v7:
time: 93.7 us; the launch traced here: 93.5 us
  Pallas kernels  92.9 us (99%)
    pallas_call x1, Pallas kernels, per_device(): pl.pallas_call(functools.partial(main_kernel, ns, nh), out_shape=(shape((...  90.2 us
    pallas_call x1, Pallas kernels, per_device(): pl.pallas_call(functools.partial(slots_kernel, ns), out_shape=(shape((wid...  2.71 us

profile of v7, /device:TPU:1, one launch (start us, length us, event | category | flops | bytes accessed | tf_op | source)
XLA Modules:
  0.0 93.5 jit_solution(14476829424941968174)
XLA Ops:
  0.6 90.2 %patch_block.1 = (s32[32,128]{1,0:T(8,128)}, bf16[64,1024]{1,0:T(8,128)(2,1)}, bf16[32,64,128]{2,1,0:T(8,128)(2,1)}, f32[16,256]{1,0:T(8,128)}, f32[1,128]{1,0:T(1,128)}) custom-call(s32[1,1024]{1,0:T(1,128)} %bitcast.5, bf16[64,4224]{1,0:T(8,128)(2,1)} %points_hbm.1, bf16[64,1024]{1,0:T(8,128)(2,1)} %cot_hbm.1, f32[1,512]{1,0:T(1,128)} %bitcast.6, ...), custom_call_target="tpu_custom_call" | custom-call | tf_op jit(solution)/shard_map/patch_block/pallas_call | solution.py:547
  90.8 2.7 %slots.1 = (bf16[64,1024]{1,0:T(8,128)(2,1)}, bf16[64,4224]{1,0:T(8,128)(2,1)}, f32[3,16,64]{2,1,0:T(8,128)}, f32[16,64]{1,0:T(8,128)}, f32[1,64]{1,0:T(1,128)}) custom-call(s32[32,128]{1,0:T(8,128)} %get-tuple-element.15.sizes_ref, bf16[32,64,128]{2,1,0:T(8,128)(2,1)} %get-tuple-element.16.back_ref, bf16[64,1024]{1,0:T(8,128)(2,1)} %get-tuple-element.17.mixed_in, ...), custom_call_target="tpu_custom_call" | custom-call | tf_op jit(solution)/shard_map/slots/pallas_call | solution.py:610

commit v8 on v7

--- a/solution.py
+++ b/solution.py
@@ -455,8 +455,8 @@
     sum_begin(0)
     wgrad_out[:, : 3 * width] = dot_nt(scaled[...], grads[...]).astype(BF16)
     wgrad_out[:, 3 * width :] = dot_nt(cot[...], context_b).astype(BF16)
+    sum_far(0)
     each(1, ns, lambda j: scan_copy(WGRAD, j).start())
-    sum_far(0)
     weighted = part_out[...].astype(F32) * gain_wide[:, :1]
     stats_out[0:1, :] = jnp.sum(weighted, axis=0, keepdims=True)
     stats_out[1:2, :] = jnp.sum(weighted * normed[...], axis=0, keepdims=True)

time: 93.7 us -> 93.6 us (level)
  no operation moved by 1% of the time
where the time goes in v8:
time: 93.6 us; the launch traced here: 93.5 us
  Pallas kernels  92.9 us (99%)
    pallas_call x1, Pallas kernels, per_device(): pl.pallas_call(functools.partial(main_kernel, ns, nh), out_shape=(shape((...  90.1 us
    pallas_call x1, Pallas kernels, per_device(): pl.pallas_call(functools.partial(slots_kernel, ns), out_shape=(shape((wid...  2.71 us

profile of v8, /device:TPU:1, one launch (start us, length us, event | category | flops | bytes accessed | tf_op | source)
XLA Modules:
  0.0 93.5 jit_solution(17599889540243970554)
XLA Ops:
  0.6 90.1 %patch_block.1 = (s32[32,128]{1,0:T(8,128)}, bf16[64,1024]{1,0:T(8,128)(2,1)}, bf16[32,64,128]{2,1,0:T(8,128)(2,1)}, f32[16,256]{1,0:T(8,128)}, f32[1,128]{1,0:T(1,128)}) custom-call(s32[1,1024]{1,0:T(1,128)} %bitcast.5, bf16[64,4224]{1,0:T(8,128)(2,1)} %points_hbm.1, bf16[64,1024]{1,0:T(8,128)(2,1)} %cot_hbm.1, f32[1,512]{1,0:T(1,128)} %bitcast.6, ...), custom_call_target="tpu_custom_call" | custom-call | tf_op jit(solution)/shard_map/patch_block/pallas_call | solution.py:547
  90.8 2.7 %slots.1 = (bf16[64,1024]{1,0:T(8,128)(2,1)}, bf16[64,4224]{1,0:T(8,128)(2,1)}, f32[3,16,64]{2,1,0:T(8,128)}, f32[16,64]{1,0:T(8,128)}, f32[1,64]{1,0:T(1,128)}) custom-call(s32[32,128]{1,0:T(8,128)} %get-tuple-element.15.sizes_ref, bf16[32,64,128]{2,1,0:T(8,128)(2,1)} %get-tuple-element.16.back_ref, bf16[64,1024]{1,0:T(8,128)(2,1)} %get-tuple-element.17.mixed_in, ...), custom_call_target="tpu_custom_call" | custom-call | tf_op jit(solution)/shard_map/slots/pallas_call | solution.py:610
